TPU v7x, 512 devices: a whole 4x4x16 slice. The times are simulated.
512 devices in a mesh: wedge: 64 (over y, z_lo, core), filt: 8 (over x, z_hi).
Axes of the slice: x: 4, y: 4, z: 16 (z_hi: 2, z_lo: 8; z = z_hi * 8 + z_lo), core: 2. Of those that a mesh axis runs over, the one named last changes fastest.
Arguments:
- x_in: bfloat16 [256, 8, 2, 1024], P('filt', None, None, 'wedge'), may hold values from -6 to 6
- h_prev: bfloat16 [256, 8, 2, 1024], P('filt', None, None, 'wedge'), may hold values from -1.25 to 1.25
- reset: int32 [8], replicated, may hold values from 0 to 1, as said below
- w_gate: bfloat16 [2, 3, 3, 256, 2, 256], P(None, None, None, 'filt'), may hold values from -0.09375 to 0.09375
- gate_bias: float32 [2, 256], P(None, 'filt'), may hold values from -3 to 3
- w_cand: bfloat16 [2, 3, 3, 256, 256], P(None, None, None, 'filt'), may hold values from -0.15625 to 0.15625
- cand_bias: float32 [256], P('filt'), may hold values from -3 to 3
- cotangent: bfloat16 [256, 8, 2, 1024], P('filt', None, None, 'wedge'), may hold values from -6 to 6
Outputs:
- h_new: bfloat16 [256, 8, 2, 1024], P('filt', None, None, 'wedge')
- grad_x: bfloat16 [256, 8, 2, 1024], P('filt', None, None, 'wedge')
- grad_h: bfloat16 [256, 8, 2, 1024], P('filt', None, None, 'wedge')
- grad_w_gate: float32 [2, 3, 3, 256, 2, 256], P(None, None, None, 'filt')
- grad_gate_bias: float32 [2, 256], P(None, 'filt')
- grad_w_cand: float32 [2, 3, 3, 256, 256], P(None, None, None, 'filt')
- grad_cand_bias: float32 [256], P('filt')
Inputs may be any that keep to these rules, and one draw needn't show every extreme that they name: `reset`: 1 marks a sample that starts a new forecast at this step; every draw has at least one sample with 1 and at least one with 0.
All inputs are finite; a program needn't handle non-finite values.
Results may differ from a plain program's by a relative error of at most 0.017.
Values may be sent and summed in bfloat16 or wider, within the bound.
A program may use at most 64 MiB of HBM per device.

v0:
```python
import jax
import jax.numpy as jnp
from jax import lax
from jax.sharding import PartitionSpec as P


def extended_2(value, sides, width):
    for axis, dim in sides:
        size, length = (lax.axis_size(axis), value.shape[dim])
        up = [(i, (i + 1) % size) for i in range(size)]
        down = [(j, i) for i, j in up]
        last = lax.slice_in_dim(value, length - width, length, axis=dim)
        leading = lax.slice_in_dim(value, 0, width, axis=dim)
        before = lax.ppermute(last, axis, up)
        after = lax.ppermute(leading, axis, down)
        value = jnp.concatenate([before, value, after], axis=dim)
    return value


def circle_pad(field):
    return jnp.pad(field, ((0, 0), (0, 0), (1, 1), (0, 0)))


def tap_columns(fields, circles, width):
    blocks = []
    for field in fields:
        padded = circle_pad(field)
        for row_step in range(3):
            for col_step in range(3):
                blocks.append(
                    padded[
                        :, :, row_step : row_step + circles, col_step : col_step + width
                    ].reshape(field.shape[0], -1)
                )
    return jnp.concatenate(blocks, axis=0)


def per_device(x_in, h_prev, reset, w_gate, gate_bias, w_cand, cand_bias, cotangent):
    chans, batch, circles, width = x_in.shape
    cells = batch * circles * width
    total_out = w_cand.shape[-1]
    keep_mask = (1 - reset).astype(jnp.bfloat16)[None, :, None, None]
    start_h = h_prev * keep_mask
    h_float = start_h.astype(jnp.float32)
    stacked = jnp.stack([x_in, start_h])
    gate_matrix = w_gate.reshape(18 * chans, -1)
    contract_rows = (((0,), (0,)), ((), ()))
    extended = extended_2(stacked, (("wedge", 4),), 1)
    outer_cols = tap_columns([extended[0], extended[1]], circles, width)
    gate_part = lax.dot_general(
        gate_matrix, outer_cols, contract_rows, preferred_element_type=jnp.float32
    )
    gate_part = gate_part.reshape(2, total_out, batch, circles, width)
    summed = lax.psum(gate_part.astype(jnp.bfloat16), "filt").astype(jnp.float32)
    own_gates = lax.dynamic_slice_in_dim(summed, lax.axis_index("filt") * chans, chans, 1)
    own_gates = own_gates + gate_bias[:, :, None, None, None]
    update = jax.nn.sigmoid(own_gates[0])
    reset_gate = jax.nn.sigmoid(own_gates[1])
    x_near = extended[0]
    gated = (reset_gate * h_float).astype(jnp.bfloat16)
    gated_near = extended_2(gated, (("wedge", 3),), 1)
    cand_cols = tap_columns([x_near, gated_near], circles, width)
    cand_part = lax.dot_general(
        w_cand.reshape(18 * chans, -1), cand_cols, contract_rows, preferred_element_type=jnp.float32
    )
    cand_part = cand_part.reshape(total_out, batch, circles, width)
    cand_pre = (
        lax.psum_scatter(
            cand_part.astype(jnp.bfloat16), "filt", scatter_dimension=0, tiled=True
        ).astype(jnp.float32)
        + cand_bias[:, None, None, None]
    )
    fresh = jnp.tanh(cand_pre)
    h_new = ((1.0 - update) * h_float + update * fresh).astype(jnp.bfloat16)
    grad_out = cotangent.astype(jnp.float32).reshape(chans, -1)
    upd_flat = update.reshape(chans, -1)
    rgate_flat = reset_gate.reshape(chans, -1)
    fresh_flat = fresh.reshape(chans, -1)
    h_flat = h_float.reshape(chans, -1)
    cand_grad = (
        (grad_out * upd_flat * (1.0 - fresh_flat * fresh_flat))
        .astype(jnp.bfloat16)
        .reshape(chans, batch, circles, width)
    )
    cand_rim = extended_2(cand_grad, (("wedge", 3),), 1)
    piece = lax.all_gather(cand_rim, "filt", axis=0, tiled=True)
    back_sum = jnp.zeros((2 * chans, cells), jnp.float32)
    count = piece.shape[0]
    padded = circle_pad(piece)
    wslice = w_cand
    for row_step in range(3):
        for col_step in range(3):
            view = padded[
                :, :, 2 - row_step : 2 - row_step + circles, 2 - col_step : 2 - col_step + width
            ].reshape(count, -1)
            tap_w = wslice[:, row_step, col_step].reshape(2 * chans, count)
            back_sum = back_sum + jnp.dot(tap_w, view, preferred_element_type=jnp.float32)
    center = piece[..., 1:-1].reshape(count, -1)
    wpart = lax.dot_general(
        cand_cols, center, (((1,), (1,)), ((), ())), preferred_element_type=jnp.float32
    )
    wgrad = wpart
    cand_back = back_sum
    cand_wgrad = wgrad
    back_x = cand_back[:chans]
    gated_grad = cand_back[chans:]
    update_term = grad_out * (fresh_flat - h_flat) * upd_flat * (1.0 - upd_flat)
    reset_term = gated_grad * h_flat * rgate_flat * (1.0 - rgate_flat)
    gate_grad = (
        jnp.stack([update_term, reset_term])
        .astype(jnp.bfloat16)
        .reshape(2, chans, batch, circles, width)
    )
    gate_rim = extended_2(gate_grad, (("wedge", 4),), 1)
    piece = lax.all_gather(gate_rim, "filt", axis=1, tiled=True)
    back_sum = jnp.zeros((2 * chans, cells), jnp.float32)
    count = piece.shape[1]
    flat_piece = piece.reshape(2 * count, batch, circles, width + 2)
    padded = circle_pad(flat_piece)
    wslice = w_gate
    for row_step in range(3):
        for col_step in range(3):
            view = padded[
                :, :, 2 - row_step : 2 - row_step + circles, 2 - col_step : 2 - col_step + width
            ].reshape(2 * count, -1)
            tap_w = wslice[:, row_step, col_step].reshape(2 * chans, 2 * count)
            back_sum = back_sum + jnp.dot(tap_w, view, preferred_element_type=jnp.float32)
    center = flat_piece[..., 1:-1].reshape(2 * count, -1)
    wpart = lax.dot_general(
        outer_cols, center, (((1,), (1,)), ((), ())), preferred_element_type=jnp.float32
    )
    wgrad = wpart.reshape(18 * chans, 2, count)
    grad_x = (back_x + back_sum[:chans]).astype(jnp.bfloat16).reshape(chans, batch, circles, width)
    keep_float = (1 - reset).astype(jnp.float32)[None, :, None, None]
    hidden_sum = grad_out * (1.0 - upd_flat) + gated_grad * rgate_flat + back_sum[chans:]
    grad_h = (hidden_sum.reshape(chans, batch, circles, width) * keep_float).astype(jnp.bfloat16)
    gate_bias_grad = jnp.sum(gate_grad.astype(jnp.float32), axis=(2, 3, 4))
    cand_bias_grad = jnp.sum(cand_grad.astype(jnp.float32), axis=(1, 2, 3))
    total_wg, total_gb, total_wc, total_cb = lax.psum(
        (
            wgrad.reshape(2, 3, 3, chans, 2, total_out),
            gate_bias_grad,
            cand_wgrad.reshape(2, 3, 3, chans, total_out),
            cand_bias_grad,
        ),
        "wedge",
    )
    return (h_new, grad_x, grad_h, total_wg, total_gb, total_wc, total_cb)


def solution(mesh):
    in_specs = (
        P("filt", None, None, "wedge"),
        P("filt", None, None, "wedge"),
        P(),
        P(None, None, None, "filt", None, None),
        P(None, "filt"),
        P(None, None, None, "filt", None),
        P("filt"),
        P("filt", None, None, "wedge"),
    )
    out_specs = (
        P("filt", None, None, "wedge"),
        P("filt", None, None, "wedge"),
        P("filt", None, None, "wedge"),
        P(None, None, None, "filt", None, None),
        P(None, "filt"),
        P(None, None, None, "filt", None),
        P("filt"),
    )
    return jax.shard_map(
        per_device, mesh=mesh, in_specs=in_specs, out_specs=out_specs, check_vma=False
    )
```

profile of v0, /device:TPU:1, one launch (start us, length us, event | category | flops | bytes accessed | tf_op | source)
XLA Modules:
  0.0 1633.0 jit_solution(3554102561225877786)
XLA Ops:
  7.2 0.7 subtract_convert_fusion
  7.9 0.9 multiply_convert_fusion.1
  8.8 0.8 pad_maximum_fusion.7
  9.6 8.8 collective-permute-start.1
  18.4 1.9 collective-permute-start
  20.4 1.2 copy.260
  21.5 7.2 collective-permute-done
  28.9 0.3 pad_slice_fusion.12
  31.0 0.4 fusion
  31.5 0.7 copy.202
  32.3 155.4 %all-reduce.10.cloned.1.call-done = bf16[2,256,8,2,16]{1,4,3,2,0:T(8,128)(2,1)} async-done(((bf16[2,256,8,2,16]{1,4,3,2,0:T(8,128)(2,1)}), bf16[2,256,8,2,16]{1,4,3,2,0:T(8,128)(2,1)}) %all-reduce.10.cloned.1.call-update) | async-done | bytes 262160 | tf_op jit(solution)/shard_map/psum | solution.py:54
  187.7 1.0 convert_add_fusion
  188.9 5.7 collective-permute-start.3
  194.6 2.3 collective-permute-start.2
  197.0 0.7 collective-permute-done.2
  198.7 0.3 fusion.1
  199.0 0.8 copy.258
  199.9 0.5 fusion.30
  200.5 0.7 copy.261
  201.3 0.7 copy.242
  202.0 104.8 %reduce-scatter.4.cloned.1.call-done = bf16[32,256]{1,0:T(8,128)(2,1)} async-done(((bf16[256,256]{1,0:T(8,128)(2,1)}), bf16[32,256]{1,0:T(8,128)(2,1)}) %reduce-scatter.4.cloned.1.call-update) | async-done | bytes 16400
  306.8 0.8 copy.259
  307.7 0.7 convert_reduce_fusion.1
  308.4 4.5 collective-permute-start.5
  312.9 2.2 collective-permute-start.4
  315.3 0.7 copy.243
  316.0 0.4 collective-permute-done.4
  316.5 0.2 copy.221
  316.7 95.8 %all_gather.6 = bf16[256,8,2,18]{3,1,2,0:T(8,128)(2,1)S(1)} all-gather(bf16[32,8,2,18]{3,1,2,0:T(8,128)(2,1)S(1)} %copy.221), channel_id=1, replica_groups=mesh['wedge'=64,'filt'=8] {'filt'}, dimensions={0}, use_global_device_ids=true | all-gather | bytes 165888 | tf_op jit(solution)/shard_map/all_gather | solution.py:86
  412.4 0.9 copy.222
  413.3 0.2 pad_slice_fusion.6
  413.7 0.2 convolution_add_fusion.7
  413.9 0.2 convolution_add_fusion.6
  414.0 0.2 convolution_add_fusion.5
  414.2 0.2 convolution_add_fusion.4
  414.4 0.2 convolution_add_fusion.3
  414.6 0.2 convolution_add_fusion.2
  414.8 0.2 convolution_add_fusion.1
  415.0 0.2 fusion.2
  415.4 12.5 collective-permute-start.7
  428.0 1.9 collective-permute-start.6
  429.9 1.0 fusion.37
  431.0 234.1 %all-reduce.5 = (f32[2,32]{1,0:T(2,128)}, f32[32]{0:T(128)}) all-reduce(f32[2,32]{1,0:T(2,128)S(1)} %convert_reduce_fusion, f32[32]{0:T(128)S(1)} %get-tuple-element.39), channel_id=1, replica_groups=mesh['wedge'=64,'filt'=8] {'wedge'}, use_global_device_ids=true, to_apply=%region_4.5 | all-reduce | flops 96 | bytes 768 | tf_op jit(solution)/shard_map/psum | solution.py:139
  665.2 0.5 copy.230
  665.7 132.2 %all_gather.7 = bf16[2,256,8,2,18]{4,2,3,0,1:T(8,128)(2,1)S(1)} all-gather(bf16[2,32,8,2,18]{4,2,3,0,1:T(8,128)(2,1)S(1)} %copy.230), channel_id=1, replica_groups=mesh['wedge'=64,'filt'=8] {'filt'}, dimensions={1}, use_global_device_ids=true | all-gather | bytes 331776 | tf_op jit(solution)/shard_map/all_gather | solution.py:115
  797.9 2.4 copy.231
  800.3 0.2 reshape.295
  800.5 0.2 pad_slice_fusion
  801.5 1.7 fusion.36
  803.2 1.3 fusion.5
  804.6 0.8 copy-done.5
  805.4 0.2 convolution_add_fusion.15
  805.6 0.2 convolution_add_fusion.14
  805.8 0.2 convolution_add_fusion.13
  806.0 0.2 convolution_add_fusion.12
  806.2 0.2 convolution_add_fusion.11
  806.4 0.2 convolution_add_fusion.10
  806.6 0.2 convolution_add_fusion.9
  806.8 0.2 fusion.3
  807.1 0.7 copy.241
  807.9 0.7 multiply_convert_fusion
  808.6 813.8 %all-reduce.12.cloned.1.call-done = (f32[2,3,3,32,2,256]{5,3,4,2,1,0:T(8,128)}, f32[2,3,3,32,256]{4,3,2,1,0:T(8,128)}) async-done(((f32[2,3,3,32,2,256]{5,3,4,2,1,0:T(8,128)}, f32[2,3,3,32,256]{4,3,2,1,0:T(8,128)}), (f32[2,3,3,32,2,256]{5,3,4,2,1,0:T(8,128)}, f32[2,3,3,32,256]{4,3,2,1,0:T(8,128)})) %all-reduce.12.cloned.1.call-update) | async-done | bytes 1769488 | tf_op jit(solution)/shard_map/psum | solution.py:139
  1622.4 3.3 copy.249
  1625.7 0.8 copy.301
  (127 shorter events, 5.0 us)
Async XLA Ops:
  7.2 21.6 %copy-start.6 = (bf16[32,8,2,16]{0,3,2,1:T(8,128)(2,1)S(1)}, bf16[32,8,2,16]{0,3,2,1:T(8,128)(2,1)}, u32[]{:S(2)}) copy-start(bf16[32,8,2,16]{0,3,2,1:T(8,128)(2,1)} %param.8) | copy-start | bytes 49156
  7.2 180.5 %all-reduce.10.cloned.1.call-start = ((), (), s32[]{:S(2)}) async-start(), calls=%async_computation.1 | async-start | bytes 524288 | tf_op jit(solution)/shard_map/psum | solution.py:54
  9.6 11.9 collective-permute-start.1
  18.4 10.3 collective-permute-start
  31.0 156.7 %copy-start.10 = (f32[2,32]{1,0:T(2,128)S(1)}, f32[2,32]{1,0:T(2,128)}, u32[]{:S(2)}) copy-start(f32[2,32]{1,0:T(2,128)} %param.12) | copy-start | bytes 772
  31.0 157.7 %copy-start.1 = (bf16[32,8,2,16]{0,3,2,1:T(8,128)(2,1)S(1)}, bf16[32,8,2,16]{0,3,2,1:T(8,128)(2,1)}, u32[]{:S(2)}) copy-start(bf16[32,8,2,16]{0,3,2,1:T(8,128)(2,1)} %param.9) | copy-start | bytes 49156
  32.2 274.6 %reduce-scatter.4.cloned.1.call-start = ((), (), s32[]{:S(2)}) async-start(), calls=%async_computation.2 | async-start | bytes 147456
  188.8 9.9 copy-start.4
  188.9 8.2 collective-permute-start.3
  194.6 3.1 collective-permute-start.2
  197.8 2.0 copy-start
  199.8 1.5 copy-start.3
  199.8 1422.6 %all-reduce.12.cloned.1.call-start = ((), (), s32[]{:S(2)}) async-start(), calls=%async_computation.3 | async-start | bytes 3538944 | tf_op jit(solution)/shard_map/psum | solution.py:139
  200.4 107.2 %copy-start.9 = (f32[32]{0:T(128)S(1)}, f32[32]{0:T(128)}, u32[]{:S(2)}) copy-start(f32[32]{0:T(128)} %param.14) | copy-start | bytes 388
  308.4 7.6 collective-permute-start.5
  312.9 3.5 collective-permute-start.4
  415.4 249.6 %collective-permute-start.7 = (bf16[2,32,8,2,1]{1,4,3,2,0:T(2,128)(2,1)S(1)}, bf16[2,32,8,2,1]{1,4,3,2,0:T(2,128)(2,1)S(1)}, u32[]{:S(2)}, u32[]{:S(2)}) collective-permute-start(bf16[2,32,8,2,1]{1,4,3,2,0:T(2,128)(2,1)S(1)} %get-tuple-element.92), channel_id=1, source_target_pairs={{8,0},{16,8},{24,16},{32,24},{40,32},{48,40},{56,48},{64,56},{72,6... | collective-permute-start | bytes 6152 | tf_op jit(solution)/shard_map/ppermute | solution.py:15
  428.0 237.1 %collective-permute-start.6 = (bf16[2,32,8,2,1]{1,4,3,2,0:T(2,128)(2,1)S(1)}, bf16[2,32,8,2,1]{1,4,3,2,0:T(2,128)(2,1)S(1)}, u32[]{:S(2)}, u32[]{:S(2)}) collective-permute-start(bf16[2,32,8,2,1]{1,4,3,2,0:T(2,128)(2,1)S(1)} %get-tuple-element.91), channel_id=1, source_target_pairs={{0,8},{8,16},{16,24},{24,32},{32,40},{40,48},{48,56},{56,64},{64,7... | collective-permute-start | bytes 6152 | tf_op jit(solution)/shard_map/ppermute | solution.py:14
  804.6 0.8 copy-start.5
  806.0 1.0 copy-start.7
  806.0 1.0 copy-start.8
  1622.4 3.3 copy-start.2
Sparse Core Ops, SparseCore 0:
  32.3 155.3 all-reduce.9
  199.9 106.8 reduce-scatter.3
  804.7 817.6 all-reduce.11
where the time goes:
time: 1630 us
  waiting for transfers between devices  1080 us (66%)
  blocking collectives  462 us (28%)
  starting transfers between devices  40 us (2%)
  local copies, waits for them, and re-layouts  20.4 us (1%)
    psum x1, waiting for transfers between devices, per_device(): lax.psum((wgrad.reshape(2, 3, 3, chans, 2, total_out), gate_bias_grad, ca...  814 us
    psum x1, blocking collectives, per_device(): lax.psum((wgrad.reshape(2, 3, 3, chans, 2, total_out), gate_bias_grad, ca...  234 us
    psum x1, waiting for transfers between devices, per_device(): lax.psum(gate_part.astype(jnp.bfloat16), 'filt').astype(jnp.float32)  155 us
    all_gather x1, blocking collectives, per_device(): piece = lax.all_gather(gate_rim, 'filt', axis=1, tiled=True)  132 us
    unnamed x4, waiting for transfers between devices  105 us
    all_gather x1, blocking collectives, per_device(): piece = lax.all_gather(cand_rim, 'filt', axis=0, tiled=True)  95.8 us
  transfers between devices with their start and end apart: 11, of which 6 were waited for; matrix products, arithmetic and copies ran while one was open for 1% of the time, Pallas kernels for 0%

commit v1 on v0

v1 whole, which is shorter than its diff:
```python
import functools

import numpy as np
import jax
import jax.numpy as jnp
from jax import lax
from jax.experimental import pallas as pl
from jax.experimental.pallas import tpu as pltpu
from jax.sharding import PartitionSpec as P

XN, ZH, YN, ZL, CN = 4, 2, 4, 8, 2
WEDGES = YN * ZL * CN
MESH = pl.DeviceIdType.MESH
BF = jnp.bfloat16
F32 = jnp.float32
NT = (((1,), (1,)), ((), ()))


def block_transpose(first, second, third):
    size = first * second * third
    order = np.arange(size).reshape(first, second, third).transpose(1, 0, 2).reshape(-1)
    matrix = np.zeros((size, size), np.float32)
    matrix[order, np.arange(size)] = 1.0
    return matrix


def two_step():
    order = np.arange(256).reshape(4, 2, 32).transpose(1, 0, 2).reshape(-1)
    matrix = np.zeros((256, 256), np.float32)
    matrix[order, np.arange(256)] = 1.0
    return matrix


def roll(v, shift):
    return pltpu.roll(v, shift, 1)


def lanes(shape):
    return lax.broadcasted_iota(jnp.int32, shape, 1)


def slot_a(shape):
    return lanes(shape) % 64 < 32


def swap(v):
    return jnp.where(slot_a(v.shape), roll(v, 96), roll(v, 32))


def dot(a, b):
    return jnp.dot(a, b, preferred_element_type=F32)


def dot_nt(a, b):
    return lax.dot_general(a, b, NT, preferred_element_type=F32)


def kernel(
    f_ref, wg_ref, wc_ref, gb_ref, cb_ref, q4_ref, q2_ref, q5_ref,
    field_ref, wgg_ref, wgc_ref, bias_ref,
    halo_l, halo_r, uf, vf, cotf, wgf, wcf, wback, wr,
    gsend, grecv, gzs, gzr, csend, crecv, czs, czr, g1, rzs, rzr, g2, ut, vt,
    blob1, blob2, r1, r2, zs, zr, zf, fin, bs, br, bs2, br2,
    s_halo, r_halo, s_g, r_g, s_c, r_c, s_a, r_a, s_b, r_b, s_w1, r_w1, s_w2, r_w2,
    s_zs, r_zs, s_zf, r_zf, s_f, r_f, s_bi, r_bi,
):
    w = lax.axis_index("wedge")
    f = lax.axis_index("filt")
    x, zh = f // ZH, f % ZH
    core, zl, yy = w % CN, (w // CN) % ZL, w // (CN * ZL)
    m = yy * CN + core

    def xpeer(d):
        return (w, ((x + d) % XN) * ZH + zh)

    zpartner = (w, x * ZH + (1 - zh))
    right = ((w + 1) % WEDGES, f)
    left = ((w + WEDGES - 1) % WEDGES, f)

    def mpeer(d):
        t = (m + d) % 8
        return ((t // CN) * ZL + zl) * CN + t % CN, f

    def lpeer(d):
        return (yy * ZL + (zl + d) % ZL) * CN + core, f

    peers = [left, right, zpartner] + [xpeer(d) for d in (1, 2, 3)]
    peers += [mpeer(d) for d in range(1, 8)] + [lpeer(d) for d in range(1, 8)]
    barrier = pltpu.get_barrier_semaphore()
    for peer in peers:
        pl.semaphore_signal(barrier, inc=1, device_id=peer, device_id_type=MESH)
    pl.semaphore_wait(barrier, len(peers))

    sends = []

    def push(src, dst, send_sem, recv_sem, peer):
        copy = pltpu.make_async_remote_copy(
            src_ref=src, dst_ref=dst, send_sem=send_sem, recv_sem=recv_sem,
            device_id=peer, device_id_type=MESH,
        )
        copy.start()
        sends.append(copy)
        return copy

    hr = push(f_ref.at[pl.ds(96, 32), :], halo_l, s_halo.at[0], r_halo.at[0], right)
    hl = push(f_ref.at[pl.ds(0, 32), :], halo_r, s_halo.at[1], r_halo.at[1], left)

    def nat(ref, a, e, lo, hi):
        return jnp.concatenate(
            [ref[((s * 3 + a) * 3 + e) * 32:((s * 3 + a) * 3 + e) * 32 + 32, lo:hi] for s in range(2)],
            axis=0,
        )

    blocks = [(e, ip) for e in range(3) for ip in range(2)]
    q4, q5 = q4_ref[...], q5_ref[...]
    for fh in range(2):
        lo = fh * 128
        lhs = jnp.concatenate(
            [
                jnp.concatenate(
                    [nat(wg_ref, a, e, g * 256 + lo, g * 256 + lo + 128) for a in (ip + 1, ip) for g in range(2)],
                    axis=1,
                )
                for e, ip in blocks
            ],
            axis=0,
        )
        out = dot(lhs, q4).astype(BF)
        wgf[2 * fh] = out[:, :256]
        wgf[2 * fh + 1] = out[:, 256:]
        masked = jnp.where(slot_a((384, 512)), out, jnp.zeros_like(out))
        zero = jnp.zeros((64, 128), BF)
        lhs = jnp.concatenate(
            [
                jnp.concatenate(
                    [zero, nat(wc_ref, ip + 1, e, lo, lo + 128), zero, nat(wc_ref, ip, e, lo, lo + 128)], axis=1
                )
                for e, ip in blocks
            ],
            axis=0,
        )
        out = dot(lhs, q4).astype(BF)
        for xl in range(2):
            cols = slice(xl * 256, xl * 256 + 256)
            for e in range(3):
                wback[2 * fh + xl, e * 256:e * 256 + 128, :] = out[e * 128:e * 128 + 128, cols]
                wback[2 * fh + xl, e * 256 + 128:e * 256 + 256, :] = masked[e * 128:e * 128 + 128, cols]
    for ref, lo, place in ((wc_ref, 0, "c"), (wg_ref, 256, "r")):
        lhs = jnp.concatenate(
            [
                jnp.concatenate([nat(ref, a, e, lo, lo + 256) for a in (ip + 1, ip)], axis=1)
                for e, ip in blocks
            ],
            axis=0,
        )
        out = dot_nt(lhs, q5).astype(BF)
        if place == "c":
            for t in range(4):
                wcf[t] = out[:, t * 128:t * 128 + 128]
        else:
            wr[...] = out

    uf[32:160, :] = f_ref[:, :128].astype(F32)
    cotf[16:144, :] = f_ref[:, 128:].astype(F32)
    hr.wait_recv()
    hl.wait_recv()
    uf[0:32, :] = halo_l[:, :128].astype(F32)
    uf[160:192, :] = halo_r[:, :128].astype(F32)
    cotf[0:16, :] = halo_l[:, 128:].astype(F32)[16:32]
    cotf[144:160, :] = halo_r[:, 128:].astype(F32)[0:16]

    lhs = jnp.concatenate([uf[e * 8:e * 8 + 176, :].astype(BF) for e in range(3)], axis=1)
    arriving = []
    for k, d in enumerate((2, 1, 3, 0)):
        t = (x + d) % XN
        part = dot(lhs, wgf[t]).astype(BF)
        gsend[t] = part
        if d:
            arriving.append(push(gsend.at[t], grecv.at[d - 1], s_g.at[d - 1], r_g.at[d - 1], xpeer(d)))
    for e in range(3):
        ut[e * 128:e * 128 + 128, :] = uf[(e + 3) * 8:(e + 3) * 8 + 128, :].T.astype(BF)
    total = gsend[x].astype(F32)
    for k, d in enumerate((2, 1, 3)):
        arriving[k].wait_recv()
        total = total + grecv[d - 1].astype(F32)
    first_z = zh == 0
    gzs[...] = jnp.where(first_z, total[:, 128:], total[:, :128]).astype(BF)
    gz = push(gzs, gzr, s_g.at[3], r_g.at[3], zpartner)
    mine = jnp.where(first_z, total[:, :128], total[:, 128:]) + gb_ref[0:1, :]
    gz.wait_recv()
    sg = jax.nn.sigmoid(mine + gzr[...].astype(F32))
    u_near = uf[8:184, :]
    vf[...] = jnp.where(slot_a((176, 128)), u_near, (sg * u_near).astype(BF).astype(F32))

    lhs = jnp.concatenate([vf[e * 8:e * 8 + 160, :].astype(BF) for e in range(3)], axis=1)
    arriving = []
    for d in (2, 1, 3, 0):
        t = (x + d) % XN
        part = dot(lhs, wcf[t]).astype(BF)
        csend[t] = part
        if d:
            arriving.append(push(csend.at[t], crecv.at[d - 1], s_c.at[d - 1], r_c.at[d - 1], xpeer(d)))
    for e in range(3):
        vt[e * 128:e * 128 + 128, :] = vf[(e + 2) * 8:(e + 2) * 8 + 128, :].T.astype(BF)
    total = csend[x].astype(F32)
    for k, d in enumerate((2, 1, 3)):
        arriving[k].wait_recv()
        total = total + crecv[d - 1].astype(F32)
    half_slot = (lanes((80, 128)) // 32) % 2
    czs[...] = jnp.where(half_slot != zh, total[:80], swap(total[80:])).astype(BF)
    cz = push(czs, czr, s_c.at[3], r_c.at[3], zpartner)
    cz.wait_recv()
    got = czr[...].astype(F32)
    total = total + jnp.concatenate([got, swap(got)], axis=0)
    cand = jnp.where(first_z, total, swap(total)) + cb_ref[0:1, :]
    fresh = jnp.tanh(cand)
    u = sg[8:168]
    h = swap(uf[16:176, :])
    cot = cotf[...]
    hn = (1.0 - u) * h + u * fresh
    cg = cot * u * (1.0 - fresh * fresh)
    upd = cot * (fresh - h) * u * (1.0 - u)
    direct = cot * (1.0 - u)
    msg = jnp.where(slot_a((160, 128)), upd, swap(cg)).astype(BF)
    g1[f] = msg
    fp = x * ZH + (1 - zh)
    az = push(g1.at[f], g1.at[f], s_a.at[0], r_a.at[0], zpartner)
    own = [push(g1.at[f], g1.at[f], s_a.at[d], r_a.at[d], xpeer(d)) for d in (2, 1, 3)]
    field_ref[:, :128] = hn[16:144].astype(BF)
    sum1 = jnp.sum(msg[16:144].astype(F32), axis=0, keepdims=True)
    az.wait_recv()
    forwarded = [push(g1.at[fp], g1.at[fp], s_a.at[3 + d], r_a.at[3 + d], xpeer(d)) for d in (2, 1, 3)]
    for copy in own + forwarded:
        copy.wait_recv()

    back = None
    for t in range(4):
        part = dot_nt(jnp.concatenate([g1[2 * t], g1[2 * t + 1]], axis=1), wback[t])
        back = part if back is None else back + part
    first = None
    second = None
    for e in range(3):
        a = back[(2 - e) * 8:(2 - e) * 8 + 144, e * 256:e * 256 + 128]
        b = back[(3 - e) * 8:(3 - e) * 8 + 128, e * 256 + 128:e * 256 + 256]
        first = a if first is None else first + a
        second = b if second is None else second + b
    r_near = sg[16:160]
    rt = (first * uf[24:168, :] * r_near * (1.0 - r_near)).astype(BF).astype(F32)
    sum2 = jnp.sum(rt[8:136], axis=0, keepdims=True)
    edge = jnp.zeros((8, 128), F32)
    rt = jnp.concatenate([edge, rt, edge], axis=0)
    rz = jnp.where(first_z, swap(rt), rt)
    rzs[...] = jnp.where(half_slot == zh, rz[:80], swap(rz[80:])).astype(BF)
    bz = push(rzs, rzr, s_b.at[0], r_b.at[0], zpartner)

    low = lanes((64, 128)) < 64
    upper = slot_a((128, 256))

    def slabs(res):
        t0, t1 = res[:, :128], res[:, 128:]
        return (
            jnp.where(low, t0[64:], t0[:64]),
            jnp.where(low, t1[64:], t1[:64]),
            jnp.where(low, t0[:64] + roll(t0[64:], 64), t1[64:] + roll(t1[:64], 64)),
        )

    for t in range(4):
        rhs = jnp.concatenate([g1[2 * t, 16:144, :], g1[2 * t + 1, 16:144, :]], axis=1)
        for e in range(3):
            rows = slice(e * 128, e * 128 + 128)
            res = jnp.where(upper, dot(ut[rows, :], rhs), dot(vt[rows, :], rhs))
            for k, slab in enumerate(slabs(res)):
                n = e * 12 + t * 3 + k
                blob1[n * 64:n * 64 + 64, :] = slab.astype(BF)
    w1 = []
    for d in range(1, 8):
        t = (m + d) % 8
        w1.append(
            push(
                blob1.at[pl.ds(pl.multiple_of(t * 288, 32), 288), :], r1.at[d - 1], s_w1.at[d - 1], r_w1.at[d - 1],
                mpeer(d),
            )
        )

    bz.wait_recv()
    got = rzr[...].astype(F32)
    full_slot = (lanes((160, 128)) // 32) % 2
    g2[x] = jnp.where(full_slot == zh, rz, jnp.concatenate([got, swap(got)], axis=0)).astype(BF)
    bx = [push(g2.at[x], g2.at[x], s_b.at[d], r_b.at[d], xpeer(d)) for d in (2, 1, 3)]
    row = lax.broadcasted_iota(jnp.int32, (8, 128), 0)
    bs[...] = jnp.where(row == 0, sum1, jnp.where(row == 1, sum2, 0.0))
    bias1 = [push(bs, br.at[d - 1], s_bi.at[d - 1], r_bi.at[d - 1], mpeer(d)) for d in range(1, 8)]
    for copy in bx:
        copy.wait_recv()

    for q in range(2):
        rhs = jnp.concatenate([g2[2 * q, 16:144, :], g2[2 * q + 1, 16:144, :]], axis=1)
        for e in range(3):
            res = dot(ut[e * 128:e * 128 + 128, :], rhs)
            for k, slab in enumerate(slabs(res)):
                n = e * 6 + q * 3 + k
                blob2[n * 64:n * 64 + 64, :] = slab.astype(BF)
    w2 = []
    for d in range(1, 8):
        t = (m + d) % 8
        w2.append(
            push(
                blob2.at[pl.ds(pl.multiple_of(t * 144, 16), 144), :], r2.at[d - 1], s_w2.at[d - 1], r_w2.at[d - 1],
                mpeer(d),
            )
        )
    back = dot_nt(jnp.concatenate([g2[t] for t in range(4)], axis=1), wr[...])
    for e in range(3):
        second = second + back[(3 - e) * 8:(3 - e) * 8 + 128, e * 128:e * 128 + 128]
    center = first[8:136]
    mixed = jnp.where(slot_a((128, 128)), center, swap(direct[16:144]) + center * sg[24:152])
    field_ref[:, 128:] = (mixed + second).astype(BF)

    t1 = blob1[pl.ds(pl.multiple_of(m * 288, 32), 288), :].astype(F32)
    for d in range(1, 8):
        w1[d - 1].wait_recv()
        t1 = t1 + r1[d - 1].astype(F32)
    for p in range(4):
        zs[p] = t1[p * 64:p * 64 + 64].astype(BF)
    b1 = bs[...]
    for d in range(1, 8):
        bias1[d - 1].wait_recv()
        b1 = b1 + br[d - 1]
    bs2[...] = b1
    bias2 = [push(bs2, br2.at[d - 1], s_bi.at[6 + d], r_bi.at[6 + d], lpeer(d)) for d in range(1, 8)]
    t2 = blob2[pl.ds(pl.multiple_of(m * 144, 16), 144), :].astype(F32)
    for d in range(1, 8):
        w2[d - 1].wait_recv()
        t2 = t2 + r2[d - 1].astype(F32)
    zs[4] = jnp.concatenate([t1[256:288], t2[:32]], axis=0).astype(BF)
    zs[5] = t2[32:96].astype(BF)
    zs[6] = jnp.concatenate([t2[96:144], jnp.zeros((16, 128), F32)], axis=0).astype(BF)
    zs[7] = jnp.zeros((64, 128), BF)
    zc = []
    for d in range(1, 8):
        t = (zl + d) % ZL
        zc.append(push(zs.at[t], zr.at[d - 1], s_zs.at[d - 1], r_zs.at[d - 1], lpeer(d)))
    total = zs[zl].astype(F32)
    for d in range(1, 8):
        zc[d - 1].wait_recv()
        total = total + zr[d - 1].astype(F32)
    zf[zl] = total.astype(BF)
    zc = [push(zf.at[zl], zf.at[zl], s_zf.at[d - 1], r_zf.at[d - 1], lpeer(d)) for d in range(1, 8)]
    b2 = bs2[...]
    for d in range(1, 8):
        bias2[d - 1].wait_recv()
        b2 = b2 + br2[d - 1]
    bias_ref[...] = b2
    for copy in zc:
        copy.wait_recv()
    for p in range(6):
        fin[m, p * 64:p * 64 + 64, :] = zf[p]
    fin[m, 384:432, :] = zf[6, 0:48, :]
    fc = [push(fin.at[m], fin.at[m], s_f.at[d - 1], r_f.at[d - 1], mpeer(d)) for d in range(1, 8)]
    for copy in fc:
        copy.wait_recv()

    def slab1(n):
        out = []
        for r in range(n * 64, n * 64 + 64, 32):
            out.append(fin[r // 288, r % 288:r % 288 + 32, :])
        return jnp.concatenate(out, axis=0)

    def slab2(n):
        out = []
        for r in range(n * 64, n * 64 + 64, 16):
            at = 288 + r % 144
            out.append(fin[r // 144, at:at + 16, :])
        return jnp.concatenate(out, axis=0)

    def put(ref, a, e, lo, value):
        for s in range(2):
            at = ((s * 3 + a) * 3 + e) * 32
            ref[at:at + 32, lo:lo + value.shape[1]] = value[s * 32:s * 32 + 32]

    for fh in range(2):
        outer = jnp.concatenate(
            [
                jnp.concatenate([slab1(e * 12 + (2 * fh + xl) * 3 + k) for xl in range(2) for k in range(2)], axis=1)
                for e in range(3)
            ],
            axis=0,
        )
        outer = dot(outer, q4)
        inner = jnp.concatenate(
            [
                jnp.concatenate([slab1(e * 12 + (2 * fh + xl) * 3 + 2) for xl in range(2)], axis=1)
                for e in range(3)
            ],
            axis=0,
        )
        inner = dot(inner, q2_ref[...])
        for e in range(3):
            rows = slice(e * 64, e * 64 + 64)
            for k, ref in enumerate((wgg_ref, wgc_ref)):
                put(ref, 2, e, fh * 128, outer[rows, k * 128:k * 128 + 128])
                put(ref, 0, e, fh * 128, outer[rows, 256 + k * 128:384 + k * 128])
                put(ref, 1, e, fh * 128, inner[rows, k * 128:k * 128 + 128])
    outer = jnp.concatenate(
        [
            jnp.concatenate([slab2(e * 6 + q * 3 + k) for q in range(2) for k in range(2)], axis=1)
            for e in range(3)
        ],
        axis=0,
    )
    outer = dot(outer, q5)
    for e in range(3):
        rows = slice(e * 64, e * 64 + 64)
        put(wgg_ref, 2, e, 256, outer[rows, :256])
        put(wgg_ref, 0, e, 256, outer[rows, 256:])
        inner = jnp.concatenate([slab2(e * 6 + q * 3 + 2) for q in range(2)], axis=1)
        put(wgg_ref, 1, e, 256, inner.astype(F32))
    for copy in sends:
        copy.wait_send()


def step_kernel(fields, wg, wc, gb, cb):
    vm = pltpu.VMEM
    dma = pltpu.SemaphoreType.DMA
    scratch = [
        vm((32, 256), BF), vm((32, 256), BF), vm((192, 128), F32), vm((176, 128), F32), vm((160, 128), F32),
        vm((4, 384, 256), BF), vm((4, 384, 128), BF), vm((4, 768, 256), BF), vm((384, 512), BF),
        vm((4, 176, 256), BF), vm((3, 176, 256), BF), vm((176, 128), BF), vm((176, 128), BF),
        vm((4, 160, 128), BF), vm((3, 160, 128), BF), vm((80, 128), BF), vm((80, 128), BF),
        vm((8, 160, 128), BF), vm((80, 128), BF), vm((80, 128), BF), vm((4, 160, 128), BF),
        vm((384, 128), BF), vm((384, 128), BF),
        vm((2304, 128), BF), vm((1152, 128), BF), vm((7, 288, 128), BF), vm((7, 144, 128), BF),
        vm((8, 64, 128), BF), vm((7, 64, 128), BF), vm((8, 64, 128), BF), vm((8, 432, 128), BF),
        vm((8, 128), F32), vm((7, 8, 128), F32), vm((8, 128), F32), vm((7, 8, 128), F32),
    ]
    for count in (2, 4, 4, 7, 4, 7, 7, 7, 7, 7, 14):
        scratch += [dma((count,)), dma((count,))]
    q4 = jnp.asarray(block_transpose(4, 4, 32), BF)
    q2 = jnp.asarray(two_step(), BF)
    q5 = jnp.asarray(block_transpose(4, 2, 64), BF)
    return pl.pallas_call(
        kernel,
        out_shape=(
            jax.ShapeDtypeStruct((128, 256), BF),
            jax.ShapeDtypeStruct((576, 512), F32),
            jax.ShapeDtypeStruct((576, 256), F32),
            jax.ShapeDtypeStruct((8, 128), F32),
        ),
        in_specs=[pl.BlockSpec(memory_space=pltpu.VMEM)] * 8,
        out_specs=[pl.BlockSpec(memory_space=pltpu.VMEM)] * 4,
        scratch_shapes=scratch,
        compiler_params=pltpu.CompilerParams(
            collective_id=0, has_side_effects=True, vmem_limit_bytes=48 * 1024 * 1024
        ),
        cost_estimate=pl.CostEstimate(flops=1_000_000_000, bytes_accessed=8_000_000, transcendentals=100_000),
    )(fields, wg, wc, gb, cb, q4, q2, q5)


def per_device(x_in, h_prev, reset, w_gate, gate_bias, w_cand, cand_bias, cotangent):
    chans, batch, circles, width = x_in.shape
    keep = (1 - reset).astype(BF)[None, :, None, None]
    start_h = h_prev * keep
    parts = jnp.stack([x_in, start_h, cotangent, jnp.zeros_like(cotangent)])
    parts = parts.reshape(2, 2, chans, batch, circles, width).transpose(5, 3, 0, 4, 1, 2)
    fields = parts.reshape(width * batch, 256)
    gb = jnp.broadcast_to(gate_bias.reshape(1, 1, 64), (8, 2, 64)).reshape(8, 128)
    cb = jnp.broadcast_to(cand_bias.reshape(1, 1, 32), (8, 4, 32)).reshape(8, 128)
    field, wgg, wgc, bias = step_kernel(
        fields, w_gate.reshape(576, 512), w_cand.reshape(576, 256), gb, cb
    )
    field = field.reshape(width, batch, 2, circles, 2, chans)
    back = lambda v: v.transpose(3, 1, 2, 0)
    h_new = back(field[:, :, 0, :, 0])
    grad_x = back(field[:, :, 1, :, 0])
    grad_h = back(field[:, :, 1, :, 1]) * keep
    sums = bias.reshape(8, 2, 2, chans).sum(axis=1)
    gb_grad = jnp.stack([sums[0, 0], sums[1, 1]])
    return (
        h_new, grad_x, grad_h, wgg.reshape(w_gate.shape), gb_grad, wgc.reshape(w_cand.shape), sums[0, 1],
    )


def solution(mesh):
    field = P("filt", None, None, "wedge")
    in_specs = (
        field, field, P(), P(None, None, None, "filt", None, None), P(None, "filt"),
        P(None, None, None, "filt", None), P("filt"), field,
    )
    out_specs = (
        field, field, field, P(None, None, None, "filt", None, None), P(None, "filt"),
        P(None, None, None, "filt", None), P("filt"),
    )
    return jax.shard_map(per_device, mesh=mesh, in_specs=in_specs, out_specs=out_specs, check_vma=False)
```

time: 1630 us -> 116 us (0.07)
  waiting for transfers between devices: 1080 us -> 0 us
  blocking collectives: 462 us -> 0 us
  Pallas kernels: 0 us -> 105 us
  starting transfers between devices: 40 us -> 0 us
    psum x2 -> x0, waiting for transfers between devices: 969 us -> none  [the longest x1 814 us: per_device(): lax.psum((wgrad.reshape(2, 3, 3, chans, 2, total_out), gate_bias_grad, ca...]
    psum x1 -> x0, blocking collectives: 234 us -> none  [per_device(): lax.psum((wgrad.reshape(2, 3, 3, chans, 2, total_out), gate_bias_grad, ca...]
    all_gather x2 -> x0, blocking collectives: 228 us -> none  [the longest x1 132 us: per_device(): piece = lax.all_gather(gate_rim, 'filt', axis=1, tiled=True)]
    unnamed x4 -> x0, waiting for transfers between devices: 105 us -> none
    pallas_call x0 -> x1, Pallas kernels: none -> 105 us  [step_kernel(): pl.pallas_call(kernel, out_shape=(jax.ShapeDtypeStruct((128, 256), BF), j...]
    ppermute x8 -> x0, starting transfers between devices: 39.9 us -> none  [the longest x4 31.5 us: extended_2(): after = lax.ppermute(leading, axis, down)]
  transfers between devices with their start and end apart: 11 -> 0, of which waited for: 6 -> 0; matrix products, arithmetic and copies ran while one was open for 1% -> 0% of each run, Pallas kernels for 0% -> 0%
where the time goes in v1:
time: 116 us
  Pallas kernels  105 us (91%)
  local copies, waits for them, and re-layouts  6.57 us (6%)
  other arithmetic  4 us (3%)
    pallas_call x1, Pallas kernels, step_kernel(): pl.pallas_call(kernel, out_shape=(jax.ShapeDtypeStruct((128, 256), BF), j...  105 us

profile of v1, /device:TPU:1, one launch (start us, length us, event | category | flops | bytes accessed | tf_op | source)
XLA Modules:
  0.0 115.9 jit_solution(8814702379435581401)
XLA Ops:
  0.6 0.0 copy-start.4
  0.6 0.7 subtract_convert_fusion
  1.4 0.8 broadcast_in_dim.21
  2.1 0.1 broadcast_in_dim.23
  2.2 0.1 pad.5.clone
  2.3 0.7 broadcast_in_dim.25
  2.9 0.1 broadcast_in_dim.26
  3.0 0.9 multiply_bitcast_fusion
  4.0 0.0 copy-start
  4.0 0.0 copy-start.1
  4.0 0.0 copy-start.2
  4.0 0.0 copy-start.3
  4.0 1.1 maximum_maximum_fusion
  5.1 0.3 copy.34
  5.4 0.2 reshape.48.f_ref
  5.5 0.0 copy-done.4
  5.5 0.1 copy.25
  5.6 0.0 copy-done
  5.7 0.0 copy-done.1
  5.7 0.0 copy-done.2
  5.7 0.0 copy-done.3
  5.7 104.6 %shard_map.162 = (bf16[128,256]{1,0:T(8,128)(2,1)S(1)}, f32[576,512]{1,0:T(8,128)S(1)}, f32[576,256]{1,0:T(8,128)S(1)}, f32[8,128]{1,0:T(8,128)S(1)}) custom-call(bf16[128,256]{1,0:T(8,128)(2,1)S(1)} %reshape.48.f_ref, bf16[576,512]{1,0:T(8,128)(2,1)S(1)} %bitcast.37, bf16[576,256]{1,0:T(8,128)(2,1)S(1)} %bitcast.38, f32[8,128]{1,0:T(8,128)S(1)} %broadcast_in_dim.24.gb_ref, ...), custom_call_target="tpu_custom_call" | custom-call | flops 1000000000 | bytes 8000000 | tf_op jit(solution)/shard_map/pallas_call | solution.py:441
  110.3 0.1 reshape.53
  110.4 0.5 slice_bitcast_fusion
  110.9 0.6 pad_maximum_fusion
  111.5 0.2 reshape.51
  111.7 0.3 fusion.2
  111.9 0.7 fusion.1
  112.6 0.7 copy_bitcast_fusion.2
  113.4 1.7 %reshape.52 = f32[2,3,3,32,2,256]{5,4,3,2,1,0:T(2,128)} reshape(f32[576,512]{1,0:T(8,128)S(1)} %get-tuple-element.12) | data formatting | bytes 2359296 | tf_op jit(solution)/shard_map/reshape | solution.py:479
  115.1 0.8 copy.36
  (4 shorter events, 0.0 us)
Async XLA Ops:
  0.6 4.9 %copy-start.4 = (bf16[2,3,3,32,2,256]{5,4,3,2,1,0:T(2,128)(2,1)S(1)}, bf16[2,3,3,32,2,256]{5,4,3,2,1,0:T(2,128)(2,1)}, u32[]{:S(2)}) copy-start(bf16[2,3,3,32,2,256]{5,4,3,2,1,0:T(2,128)(2,1)} %param.14) | copy-start | bytes 1769476
  4.0 1.7 %copy-start = (bf16[2,3,3,32,256]{4,3,2,1,0:T(8,128)(2,1)S(1)}, bf16[2,3,3,32,256]{4,3,2,1,0:T(8,128)(2,1)}, u32[]{:S(2)}) copy-start(bf16[2,3,3,32,256]{4,3,2,1,0:T(8,128)(2,1)} %param.16) | copy-start | bytes 884740
  4.0 1.7 %copy-start.1 = (bf16[512,512]{1,0:T(8,128)(2,1)S(1)}, bf16[512,512]{1,0:T(8,128)(2,1)}, u32[]{:S(2)}) copy-start(bf16[512,512]{1,0:T(8,128)(2,1)} %constant.14.clone.q5_ref) | copy-start | bytes 1572868
  4.0 1.7 %copy-start.2 = (bf16[512,512]{1,0:T(8,128)(2,1)S(1)}, bf16[512,512]{1,0:T(8,128)(2,1)}, u32[]{:S(2)}) copy-start(bf16[512,512]{1,0:T(8,128)(2,1)} %constant.12.clone.q4_ref) | copy-start | bytes 1572868
  4.0 1.7 %copy-start.3 = (bf16[256,256]{1,0:T(8,128)(2,1)S(1)}, bf16[256,256]{1,0:T(8,128)(2,1)}, u32[]{:S(2)}) copy-start(bf16[256,256]{1,0:T(8,128)(2,1)} %constant.13.clone.q2_ref) | copy-start | bytes 393220

commit v2 on v0

v2 whole, which is shorter than its diff:
```python
import numpy as np
import jax
import jax.numpy as jnp
from jax import lax
from jax.experimental import pallas as pl
from jax.experimental.pallas import tpu as pltpu
from jax.sharding import PartitionSpec as P

XN, ZH, YN, ZL, CN = 4, 2, 4, 8, 2
WEDGES = YN * ZL * CN
COPIES = 104
MESH = pl.DeviceIdType.MESH
BF = jnp.bfloat16
F32 = jnp.float32
NT = (((1,), (1,)), ((), ()))


def block_transpose(first, second, third):
    size = first * second * third
    order = np.arange(size).reshape(first, second, third).transpose(1, 0, 2).reshape(-1)
    matrix = np.zeros((size, size), np.float32)
    matrix[order, np.arange(size)] = 1.0
    return matrix


def row_order():
    order = np.arange(128).reshape(8, 16).T.reshape(-1)
    matrix = np.zeros((128, 128), np.float32)
    matrix[np.arange(128), order] = 1.0
    return matrix


def roll(v, shift):
    return pltpu.roll(v, shift, 1)


def slot_a(shape):
    return lax.broadcasted_iota(jnp.int32, shape, 1) % 64 < 32


def swap(v):
    return jnp.where(slot_a(v.shape), roll(v, 96), roll(v, 32))


def dot(a, b):
    return jnp.dot(a, b, preferred_element_type=F32)


def dot_nt(a, b):
    return lax.dot_general(a, b, NT, preferred_element_type=F32)


def tiles(ref):
    return jnp.concatenate([ref[t] for t in range(4)], axis=1)


def taps(ref, start, rows):
    return jnp.concatenate([ref[start + e * 8:start + e * 8 + rows, :].astype(BF) for e in range(3)], axis=1)


def shifted(v, start, rows):
    out = None
    for e in range(3):
        part = v[start + (2 - e) * 8:start + (2 - e) * 8 + rows, e * 128:e * 128 + 128]
        out = part if out is None else out + part
    return out


def kernel(
    reset_ref, x_ref, h_ref, ct_ref, wg_ref, wc_ref, gb_ref, cb_ref, q5_ref, pm_ref,
    field_ref, fin_a, fin_r, bias_ref,
    f_ref, halo_l, halo_r, uf, near_l, near_r, far, hp, cp, wch, w_upd, w_res, w_cx, w_ch,
    bz_s, bz_r, gs_r, gr_r, gs_u, gr_u, zs_r, zr_r, zs_u, zr_u, gpf, cs, cr,
    g1c, g1u, g2, ut, vt, blob_a, blob_r, core_a, mid_a, y_a, m_r,
    zs_a, zq_a, zf_a, zs_b, zq_b, zf_b, bs, br, bs2, br2,
    send_sems, recv_sems,
):
    w = lax.axis_index("wedge")
    f = lax.axis_index("filt")
    x, zh = f // ZH, f % ZH
    core, zl, yy = w % CN, (w // CN) % ZL, w // (CN * ZL)
    m = yy * CN + core
    first_z = zh == 0
    fp = x * ZH + (1 - zh)
    after, before = (w + 1) % WEDGES, (w + WEDGES - 1) % WEDGES

    def xpeer(d):
        return (w, ((x + d) % XN) * ZH + zh)

    def at_y(t, c):
        return (t * ZL + zl) * CN + c, f

    def mpeer(d):
        t = (m + d) % 8
        return at_y(t // CN, t % CN)

    def ypeer(d):
        return at_y((yy + d) % YN, core)

    def lpeer(d):
        return (yy * ZL + (zl + d) % ZL) * CN + core, f

    partner = (w, fp)
    other_core = at_y(yy, 1 - core)
    peers = [(after, f), (before, f), (after, fp), (before, fp), partner] + [xpeer(d) for d in (1, 2, 3)]
    peers += [mpeer(d) for d in range(1, 8)] + [lpeer(d) for d in range(1, 8)]
    barrier = pltpu.get_barrier_semaphore()
    for peer in peers:
        pl.semaphore_signal(barrier, inc=1, device_id=peer, device_id_type=MESH)

    def own_a(v):
        return jnp.where(first_z, v, swap(v))

    def own_b(v):
        return jnp.where(first_z, swap(v), v)

    order = pm_ref[...]
    kept = jnp.concatenate(
        [h_ref[b:b + 1].astype(F32) * (1 - reset_ref[b]).astype(F32) for b in range(8)], axis=0
    )
    near, wide = [], []
    for i in range(2):
        hidden = kept[:, i].reshape(128, 32)
        near += [x_ref[:, i].reshape(128, 32).astype(F32), hidden]
        wide += [ct_ref[:, i].reshape(128, 32).astype(F32), hidden]
    own_u = dot(order, jnp.concatenate(near, axis=1).astype(BF))
    own_c = dot(order, jnp.concatenate(wide, axis=1).astype(BF))
    f_ref[:, :128] = own_u.astype(BF)
    f_ref[:, 128:] = own_c.astype(BF)
    uf[32:160, :] = own_u
    row = lax.broadcasted_iota(jnp.int32, (8, 128), 0)
    bias_rows = [jnp.concatenate([v] * 4, axis=1) for v in (gb_ref[0:1, :], gb_ref[1:2, :], cb_ref[...])]
    bias_rows = jnp.where(row == 0, bias_rows[0], jnp.where(row == 1, bias_rows[1], bias_rows[2]))
    bz_s[...] = jnp.where(slot_a((8, 128)) == first_z, bias_rows, 0.0)
    pl.semaphore_wait(barrier, len(peers))

    sends = []

    def push(src, dst, peer):
        at = len(sends)
        copy = pltpu.make_async_remote_copy(
            src_ref=src, dst_ref=dst, send_sem=send_sems.at[at], recv_sem=recv_sems.at[at],
            device_id=peer, device_id_type=MESH,
        )
        copy.start()
        sends.append(copy)
        return copy

    def landed(copies):
        for copy in copies:
            copy.wait_recv()

    right, left = pl.ds(96, 32), pl.ds(0, 32)
    second = pl.ds(128, 128)
    halo = [
        push(f_ref.at[right, :], halo_l, (after, f)),
        push(f_ref.at[left, :], halo_r, (before, f)),
    ]
    pair = [
        push(f_ref.at[right, second], near_l, (after, fp)),
        push(f_ref.at[left, second], near_r, (before, fp)),
        push(f_ref.at[:, second], far, partner),
        push(bz_s, bz_r, partner),
    ]
    pair_w = push(wc_ref.at[pl.ds(288, 288), :], wch.at[zh], partner)
    wch[zh] = wc_ref[288:576, :]
    q5 = q5_ref[...]

    def arrange(nat, out_ref):
        lhs = jnp.concatenate(
            [
                jnp.concatenate([nat(a, e) for a in (ip + 1, ip)], axis=1)
                for e in range(3)
                for ip in range(2)
            ],
            axis=0,
        )
        out = dot_nt(lhs, q5).astype(BF)
        for t in range(4):
            out_ref[t] = out[:, t * 128:t * 128 + 128]

    def both(ref, lo):
        def nat(a, e):
            rows = [((s * 3 + a) * 3 + e) * 32 for s in range(2)]
            return jnp.concatenate([ref[r:r + 32, lo:lo + 256] for r in rows], axis=0)

        return nat

    def input_only(a, e):
        at = (a * 3 + e) * 32
        return jnp.concatenate([wc_ref[at:at + 32, :], jnp.zeros((32, 256), BF)], axis=0)

    def pair_hidden(a, e):
        at = (a * 3 + e) * 32
        return jnp.concatenate([wch[0, at:at + 32, :], wch[1, at:at + 32, :]], axis=0)

    arrange(both(wg_ref, 256), w_res)
    arrange(both(wg_ref, 0), w_upd)
    arrange(input_only, w_cx)
    landed(halo)
    uf[0:32, :] = halo_l[:, :128].astype(F32)
    uf[160:192, :] = halo_r[:, :128].astype(F32)

    lhs = taps(uf, 0, 176)
    res = []
    for d in (2, 1, 3, 0):
        t = (x + d) % XN
        gs_r[t] = dot(lhs, w_res[t]).astype(BF)
        if d:
            res.append(push(gs_r.at[t], gr_r.at[d - 1], xpeer(d)))
    lhs = taps(uf, 8, 160)
    upd = []
    for d in (2, 1, 3, 0):
        t = (x + d) % XN
        gs_u[t] = dot(lhs, jnp.concatenate([w_upd[t], w_cx[t]], axis=1)).astype(BF)
        if d:
            upd.append(push(gs_u.at[t], gr_u.at[d - 1], xpeer(d)))
    sum_r = gs_r[x].astype(F32)
    landed(res)
    for d in range(3):
        sum_r = sum_r + gr_r[d].astype(F32)
    zs_r[...] = sum_r.astype(BF)
    zr = push(zs_r, zr_r, partner)
    sum_u = gs_u[x].astype(F32)
    landed(upd)
    for d in range(3):
        sum_u = sum_u + gr_u[d].astype(F32)
    zs_u[...] = sum_u.astype(BF)
    zu = push(zs_u, zr_u, partner)

    for e in range(3):
        ut[e * 128:e * 128 + 128, :] = uf[(e + 3) * 8:(e + 3) * 8 + 128, :].T.astype(BF)
    landed(pair)
    biases = bz_s[...] + bz_r[...]
    for lo, mine, theirs in (
        (0, halo_l[:, 128:], near_l[...]), (32, f_ref[:, 128:], far[...]), (160, halo_r[:, 128:], near_r[...])
    ):
        mine, theirs = mine.astype(F32), theirs.astype(F32)
        block_0 = jnp.where(first_z, mine, theirs)
        block_1 = jnp.where(first_z, theirs, mine)
        at = slot_a(mine.shape)
        hp[lo:lo + mine.shape[0], :] = jnp.where(at, swap(block_0), block_1)
        cp[lo:lo + mine.shape[0], :] = jnp.where(at, block_0, swap(block_1))
    pair_w.wait_recv()
    arrange(pair_hidden, w_ch)

    zr.wait_recv()
    r = jax.nn.sigmoid(sum_r + zr_r[...].astype(F32) + biases[1:2, :])
    gp = (r * hp[8:184, :]).astype(BF).astype(F32)
    gpf[...] = gp

    lhs = taps(gpf, 0, 160)
    cand = []
    for d in (2, 1, 3, 0):
        t = (x + d) % XN
        cs[t] = dot(lhs, w_ch[t]).astype(BF)
        if d:
            cand.append(push(cs.at[t], cr.at[d - 1], xpeer(d)))
    own_v = jnp.where(slot_a((176, 128)), uf[8:184, :], own_b(gp))
    for e in range(3):
        vt[e * 128:e * 128 + 128, :] = own_v[(e + 2) * 8:(e + 2) * 8 + 128].T.astype(BF)
    zu.wait_recv()
    sum_u = sum_u + zr_u[...].astype(F32)
    u = jax.nn.sigmoid(sum_u[:, :128] + biases[0:1, :])
    pre = sum_u[:, 128:] + biases[2:3, :] + cs[x].astype(F32)
    landed(cand)
    for d in range(3):
        pre = pre + cr[d].astype(F32)
    fresh = jnp.tanh(pre)
    h = hp[16:176, :]
    cot = cp[16:176, :]
    cg = (cot * u * (1.0 - fresh * fresh)).astype(BF)
    g1c[x] = cg
    got_c = [push(g1c.at[x], g1c.at[x], xpeer(d)) for d in (2, 1, 3)]
    ug = (cot * (fresh - h) * u * (1.0 - u)).astype(BF)
    g1u[x] = ug
    got_u = [push(g1u.at[x], g1u.at[x], xpeer(d)) for d in (2, 1, 3)]
    direct = (cot * (1.0 - u))[16:144]
    hn = ((1.0 - u) * h + u * fresh)[16:144]
    field_ref[:, :128] = own_a(hn).astype(BF)
    sum_c = jnp.sum(cg[16:144].astype(F32), axis=0, keepdims=True)
    sum_g = jnp.sum(ug[16:144].astype(F32), axis=0, keepdims=True)

    landed(got_c)
    grads = tiles(g1c)
    gg = shifted(dot_nt(grads, tiles(w_ch)), 0, 144)
    r_near = r[16:160]
    rt = (gg * hp[24:168, :] * r_near * (1.0 - r_near)).astype(BF).astype(F32)
    edge = jnp.zeros((8, 128), F32)
    g2[x] = jnp.concatenate([edge, rt, edge], axis=0).astype(BF)
    got_r = [push(g2.at[x], g2.at[x], xpeer(d)) for d in (2, 1, 3)]
    sum_q = jnp.sum(rt[8:136], axis=0, keepdims=True)
    bs[...] = jnp.where(row == 0, sum_g, jnp.where(row == 1, sum_q, jnp.where(row == 2, sum_c, 0.0)))
    bias1 = [push(bs, br.at[d - 1], mpeer(d)) for d in range(1, 8)]

    low = lax.broadcasted_iota(jnp.int32, (64, 128), 1) < 64

    def weight_grad(left_ref, grad_ref, out_ref, start):
        left_rows = left_ref[...]
        for q in range(2):
            rhs = jnp.concatenate([grad_ref[2 * q, 16:144, :], grad_ref[2 * q + 1, 16:144, :]], axis=1)
            product = dot(left_rows, rhs)
            for e in range(3):
                t0 = product[e * 128:e * 128 + 128, :128]
                t1 = product[e * 128:e * 128 + 128, 128:]
                slabs = (
                    jnp.where(low, t0[64:], t0[:64]),
                    jnp.where(low, t1[64:], t1[:64]),
                    jnp.where(low, t0[:64] + roll(t0[64:], 64), t1[64:] + roll(t1[:64], 64)),
                )
                for k, slab in enumerate(slabs):
                    n = (start + e * 6 + q * 3 + k) * 64
                    out_ref[n:n + 64, :] = slab.astype(BF)

    def chunk(t, rows):
        return pl.ds(pl.multiple_of(t * rows, 16), rows)

    weight_grad(vt, g1c, blob_a, 0)
    landed(got_u)
    weight_grad(ut, g1u, blob_a, 18)
    half = [push(blob_a.at[chunk(t * CN + 1 - core, 288), :], core_a.at[t], other_core) for t in range(4)]
    total = shifted(dot_nt(grads, tiles(w_cx)), 8, 128) + shifted(dot_nt(tiles(g1u), tiles(w_upd)), 8, 128)
    landed(half)
    for t in range(4):
        mid_a[t] = (blob_a[chunk(t * CN + core, 288), :].astype(F32) + core_a[t].astype(F32)).astype(BF)
    over_y = [push(mid_a.at[(yy + d) % YN], y_a.at[d - 1], ypeer(d)) for d in (2, 1, 3)]

    landed(got_r)
    weight_grad(ut, g2, blob_r, 0)
    over_m = [push(blob_r.at[chunk((m + d) % 8, 144), :], m_r.at[d - 1], mpeer(d)) for d in range(1, 8)]
    total = total + shifted(dot_nt(tiles(g2), tiles(w_res)), 8, 128)
    hidden = own_b(direct + gg[8:136] * r[24:152])
    field_ref[:, 128:] = jnp.where(slot_a((128, 128)), total, hidden + total).astype(BF)

    acc = mid_a[yy].astype(F32)
    landed(over_y)
    for d in range(3):
        acc = acc + y_a[d].astype(F32)
    for p in range(6):
        zs_a[p] = acc[p * 48:p * 48 + 48].astype(BF)
    for p in (6, 7):
        zs_a[p] = jnp.zeros((48, 128), BF)
    over_za = [push(zs_a.at[(zl + d) % ZL], zq_a.at[d - 1], lpeer(d)) for d in range(1, 8)]
    b1 = bs[...]
    landed(bias1)
    for d in range(7):
        b1 = b1 + br[d]
    bs2[...] = b1
    bias2 = [push(bs2, br2.at[d - 1], lpeer(d)) for d in range(1, 8)]
    acc = blob_r[chunk(m, 144), :].astype(F32)
    landed(over_m)
    for d in range(7):
        acc = acc + m_r[d].astype(F32)
    for p in range(4):
        zs_b[p] = acc[p * 32:p * 32 + 32].astype(BF)
    zs_b[4] = jnp.concatenate([acc[128:144], jnp.zeros((16, 128), F32)], axis=0).astype(BF)
    for p in (5, 6, 7):
        zs_b[p] = jnp.zeros((32, 128), BF)
    over_zb = [push(zs_b.at[(zl + d) % ZL], zq_b.at[d - 1], lpeer(d)) for d in range(1, 8)]

    def own_sum(mine, came, copies, out):
        value = mine[zl].astype(F32)
        landed(copies)
        for d in range(7):
            value = value + came[d].astype(F32)
        out[zl] = value.astype(BF)
        return [push(out.at[zl], out.at[zl], lpeer(d)) for d in range(1, 8)]

    back_a = own_sum(zs_a, zq_a, over_za, zf_a)
    back_b = own_sum(zs_b, zq_b, over_zb, zf_b)

    def spread(fin):
        to_y = [push(fin.at[m], fin.at[m], ypeer(d)) for d in (2, 1, 3)]
        return to_y, [push(fin.at[m], fin.at[m], other_core)]

    def forward(fin, to_y, rest):
        for copy, d in zip(to_y, (2, 1, 3)):
            copy.wait_recv()
            at = ((yy + YN - d) % YN) * CN + core
            rest.append(push(fin.at[at], fin.at[at], other_core))

    landed(back_a)
    for p in range(6):
        fin_a[m, p * 48:p * 48 + 48, :] = zf_a[p]
    to_ya, rest_a = spread(fin_a)
    landed(back_b)
    for p in range(4):
        fin_r[m, p * 32:p * 32 + 32, :] = zf_b[p]
    fin_r[m, 128:144, :] = zf_b[4, 0:16, :]
    to_yr, rest_r = spread(fin_r)
    b2 = bs2[...]
    landed(bias2)
    for d in range(7):
        b2 = b2 + br2[d]
    bias_ref[...] = own_a(b2)
    forward(fin_a, to_ya, rest_a)
    forward(fin_r, to_yr, rest_r)
    landed(rest_a)
    landed(rest_r)
    for copy in sends:
        copy.wait_send()


def finish(
    reset_ref, field_ref, fin_a, fin_r, bias_ref, q5_ref, pm_ref,
    hn_ref, gx_ref, gh_ref, wgg_ref, gb_ref, wgc_ref, cb_ref,
):
    rows = dot(pm_ref[...], field_ref[...])
    for i in range(2):
        hn_ref[:, i] = rows[:, i * 64:i * 64 + 32].reshape(8, 16, 32).astype(BF)
        gx_ref[:, i] = rows[:, 128 + i * 64:160 + i * 64].reshape(8, 16, 32).astype(BF)
        value = rows[:, 160 + i * 64:192 + i * 64].reshape(8, 16, 32)
        for b in range(8):
            gh_ref[b, i] = (value[b] * (1 - reset_ref[b]).astype(F32)).astype(BF)
    sums = bias_ref[...]
    sums = sums + roll(sums, 64)
    gb_ref[...] = sums[0:2, 0:32]
    cb_ref[...] = sums[2:3, 0:32]

    def slab(fin, size, step, n):
        pieces = [fin[r // size, r % size:r % size + step, :] for r in range(n * 64, n * 64 + 64, step)]
        return jnp.concatenate(pieces, axis=0)

    def put(gate, a, e, value):
        for s in range(2):
            part = value[s * 32:s * 32 + 32]
            if gate is None:
                wgc_ref[s, a, e] = part
            else:
                wgg_ref[s, a, e, :, gate, :] = part

    q5 = q5_ref[...]
    for gate, fin, size, step, start in (
        (None, fin_a, 288, 32, 0), (0, fin_a, 288, 32, 18), (1, fin_r, 144, 16, 0)
    ):
        def get(e, q, k):
            return slab(fin, size, step, start + e * 6 + q * 3 + k)

        outer = jnp.concatenate(
            [
                jnp.concatenate([get(e, q, k) for q in range(2) for k in range(2)], axis=1)
                for e in range(3)
            ],
            axis=0,
        )
        outer = dot(outer, q5)
        for e in range(3):
            at = slice(e * 64, e * 64 + 64)
            put(gate, 2, e, outer[at, :256])
            put(gate, 0, e, outer[at, 256:])
            inner = jnp.concatenate([get(e, q, 2) for q in range(2)], axis=1)
            put(gate, 1, e, inner.astype(F32))


def per_device(x_in, h_prev, reset, w_gate, gate_bias, w_cand, cand_bias, cotangent):
    def bf(*shape):
        return pltpu.VMEM(shape, BF)

    def f32(*shape):
        return pltpu.VMEM(shape, F32)

    scratch = [
        bf(128, 256), bf(32, 256), bf(32, 256), f32(192, 128), bf(32, 128), bf(32, 128), bf(128, 128),
        f32(192, 128), f32(192, 128), bf(2, 288, 256),
        bf(4, 384, 128), bf(4, 384, 128), bf(4, 384, 128), bf(4, 384, 128),
        f32(8, 128), f32(8, 128), bf(4, 176, 128), bf(3, 176, 128), bf(4, 160, 256), bf(3, 160, 256),
        bf(176, 128), bf(176, 128), bf(160, 256), bf(160, 256), f32(176, 128), bf(4, 160, 128), bf(3, 160, 128),
        bf(4, 160, 128), bf(4, 160, 128), bf(4, 160, 128), bf(384, 128), bf(384, 128),
        bf(2304, 128), bf(1152, 128), bf(4, 288, 128), bf(4, 288, 128), bf(3, 288, 128), bf(7, 144, 128),
        bf(8, 48, 128), bf(7, 48, 128), bf(8, 48, 128), bf(8, 32, 128), bf(7, 32, 128), bf(8, 32, 128),
        f32(8, 128), f32(7, 8, 128), f32(8, 128), f32(7, 8, 128),
        pltpu.SemaphoreType.DMA((COPIES,)), pltpu.SemaphoreType.DMA((COPIES,)),
    ]
    q5 = jnp.asarray(block_transpose(4, 2, 64), BF)
    rows_in = jnp.asarray(row_order(), BF)
    rows_out = jnp.asarray(row_order().T, BF)
    near = lambda v: v.transpose(1, 2, 3, 0)
    smem = pl.BlockSpec(memory_space=pltpu.SMEM)
    whole = pl.BlockSpec(memory_space=pltpu.VMEM)
    field, fin_a, fin_r, bias = pl.pallas_call(
        kernel,
        out_shape=(
            jax.ShapeDtypeStruct((128, 256), BF),
            jax.ShapeDtypeStruct((8, 288, 128), BF),
            jax.ShapeDtypeStruct((8, 144, 128), BF),
            jax.ShapeDtypeStruct((8, 128), F32),
        ),
        in_specs=[smem] + [whole] * 9,
        out_specs=[whole] * 4,
        scratch_shapes=scratch,
        compiler_params=pltpu.CompilerParams(
            collective_id=0, has_side_effects=True, vmem_limit_bytes=48 * 1024 * 1024
        ),
        cost_estimate=pl.CostEstimate(flops=1_000_000_000, bytes_accessed=8_000_000, transcendentals=100_000),
    )(
        reset, near(x_in), near(h_prev), near(cotangent), w_gate.reshape(576, 512), w_cand.reshape(576, 256),
        gate_bias, cand_bias.reshape(1, 32), q5, rows_in,
    )
    shape = jax.ShapeDtypeStruct((8, 2, 16, 32), BF)
    h_new, grad_x, grad_h, wgg, gb, wgc, cb = pl.pallas_call(
        finish,
        out_shape=(
            shape, shape, shape,
            jax.ShapeDtypeStruct(w_gate.shape, F32), jax.ShapeDtypeStruct((2, 32), F32),
            jax.ShapeDtypeStruct(w_cand.shape, F32), jax.ShapeDtypeStruct((1, 32), F32),
        ),
        in_specs=[smem] + [whole] * 6,
        out_specs=[whole] * 7,
        compiler_params=pltpu.CompilerParams(vmem_limit_bytes=32 * 1024 * 1024),
    )(reset, field, fin_a, fin_r, bias, q5, rows_out)
    back = lambda v: v.transpose(3, 0, 1, 2)
    return back(h_new), back(grad_x), back(grad_h), wgg, gb, wgc, cb.reshape(32)


def solution(mesh):
    field = P("filt", None, None, "wedge")
    in_specs = (
        field, field, P(), P(None, None, None, "filt", None, None), P(None, "filt"),
        P(None, None, None, "filt", None), P("filt"), field,
    )
    out_specs = (
        field, field, field, P(None, None, None, "filt", None, None), P(None, "filt"),
        P(None, None, None, "filt", None), P("filt"),
    )
    return jax.shard_map(per_device, mesh=mesh, in_specs=in_specs, out_specs=out_specs, check_vma=False)
```

time: 1630 us -> 94.5 us (0.06)
  waiting for transfers between devices: 1080 us -> 0 us
  blocking collectives: 462 us -> 0 us
  Pallas kernels: 0 us -> 92.2 us
  starting transfers between devices: 40 us -> 0 us
  local copies, waits for them, and re-layouts: 20.4 us -> 1.28 us
    psum x2 -> x0, waiting for transfers between devices: 969 us -> none  [the longest x1 814 us: per_device(): lax.psum((wgrad.reshape(2, 3, 3, chans, 2, total_out), gate_bias_grad, ca...]
    psum x1 -> x0, blocking collectives: 234 us -> none  [per_device(): lax.psum((wgrad.reshape(2, 3, 3, chans, 2, total_out), gate_bias_grad, ca...]
    all_gather x2 -> x0, blocking collectives: 228 us -> none  [the longest x1 132 us: per_device(): piece = lax.all_gather(gate_rim, 'filt', axis=1, tiled=True)]
    unnamed x4 -> x0, waiting for transfers between devices: 105 us -> none
    pallas_call x0 -> x2, Pallas kernels: none -> 92.2 us  [the longest x1 89.8 us: per_device(): pl.pallas_call(kernel, out_shape=(jax.ShapeDtypeStruct((128, 256), BF), j...]
    ppermute x8 -> x0, starting transfers between devices: 39.9 us -> none  [the longest x4 31.5 us: extended_2(): after = lax.ppermute(leading, axis, down)]
  transfers between devices with their start and end apart: 11 -> 0, of which waited for: 6 -> 0; matrix products, arithmetic and copies ran while one was open for 1% -> 0% of each run, Pallas kernels for 0% -> 0%
where the time goes in v2:
time: 94.5 us; the launch traced here: 94.3 us
  Pallas kernels  92.2 us (98%)
  local copies, waits for them, and re-layouts  1.28 us (1%)
    pallas_call x1, Pallas kernels, per_device(): pl.pallas_call(kernel, out_shape=(jax.ShapeDtypeStruct((128, 256), BF), j...  89.8 us
    pallas_call x1, Pallas kernels, per_device(): pl.pallas_call(finish, out_shape=(shape, shape, shape, jax.ShapeDtypeStru...  2.43 us

profile of v2, /device:TPU:1, one launch (start us, length us, event | category | flops | bytes accessed | tf_op | source)
XLA Modules:
  0.0 94.3 jit_solution(16891105922808825651)
XLA Ops:
  0.6 0.0 copy-start
  0.6 0.0 copy-start.9
  0.7 0.0 copy-start.2
  0.7 0.0 copy-start.6
  0.7 0.0 copy-start.8
  0.7 0.0 copy-start.3
  0.7 0.0 copy-start.7
  0.7 0.0 copy-start.5
  0.7 0.0 copy-start.4
  0.7 1.2 %copy.18 = bf16[72,8,2,256]{3,1,2,0:T(8,128)(2,1)S(1)} copy(bf16[72,8,2,256]{3,2,1,0:T(2,128)(2,1)} %bitcast.18) | data formatting | bytes 1179648
  2.0 0.0 copy-done
  2.0 0.0 copy-done.9
  2.0 0.0 copy-done.2
  2.0 0.0 copy-done.6
  2.0 0.0 copy-done.8
  2.0 0.0 copy-done.3
  2.0 0.0 copy-done.7
  2.0 0.0 copy-done.5
  2.0 0.0 copy-done.4
  2.1 0.0 copy-start.1
  2.1 89.8 %shard_map.162 = (bf16[128,256]{1,0:T(8,128)(2,1)S(1)}, bf16[8,288,128]{2,1,0:T(8,128)(2,1)S(1)}, bf16[8,144,128]{2,1,0:T(8,128)(2,1)S(1)}, f32[8,128]{1,0:T(8,128)S(1)}) custom-call(s32[8]{0:T(128)S(1)} %copy-done.2, bf16[8,2,16,32]{3,2,1,0:T(8,128)(2,1)S(1)} %bitcast.14, bf16[8,2,16,32]{3,2,1,0:T(8,128)(2,1)S(1)} %bitcast.15, ...), custom_call_target="tpu_custom_call" | custom-call | flops 1000000000 | bytes 8000000 | tf_op jit(solution)/shard_map/pallas_call | solution.py:480
  91.9 0.0 copy-done.1
  91.9 2.4 %shard_map.163 = (bf16[8,2,16,32]{3,2,1,0:T(8,128)(2,1)}, bf16[8,2,16,32]{3,2,1,0:T(8,128)(2,1)}, bf16[8,2,16,32]{3,2,1,0:T(8,128)(2,1)}, f32[2,3,3,32,2,256]{5,...) custom-call(s32[8]{0:T(128)S(1)} %copy-done.2, ...), custom_call_target="tpu_custom_call" | custom-call | tf_op jit(solution)/shard_map/pallas_call | solution.py:500
Async XLA Ops:
  0.6 1.3 %copy-start = (bf16[512,512]{1,0:T(8,128)(2,1)S(1)}, bf16[512,512]{1,0:T(8,128)(2,1)}, u32[]{:S(2)}) copy-start(bf16[512,512]{1,0:T(8,128)(2,1)} %constant.6.clone.q5_ref) | copy-start | bytes 1572868
  0.6 1.3 %copy-start.9 = (bf16[128,128]{1,0:T(8,128)(2,1)S(1)}, bf16[128,128]{1,0:T(8,128)(2,1)}, u32[]{:S(2)}) copy-start(bf16[128,128]{1,0:T(8,128)(2,1)} %constant.7.clone.pm_ref) | copy-start | bytes 98308
  0.7 1.3 %copy-start.2 = (s32[8]{0:T(128)S(1)}, s32[8]{0:T(128)}, u32[]{:S(2)}) copy-start(s32[8]{0:T(128)} %reset_ref.3) | copy-start | bytes 100
  0.7 1.3 %copy-start.6 = (bf16[32,8,2,16]{0,3,2,1:T(8,128)(2,1)S(1)}, bf16[32,8,2,16]{0,3,2,1:T(8,128)(2,1)}, u32[]{:S(2)}) copy-start(bf16[32,8,2,16]{0,3,2,1:T(8,128)(2,1)} %param.18) | copy-start | bytes 49156
  0.7 1.3 %copy-start.8 = (f32[32]{0:T(128)S(1)}, f32[32]{0:T(128)}, u32[]{:S(2)}) copy-start(f32[32]{0:T(128)} %param.17) | copy-start | bytes 388
  0.7 1.3 %copy-start.3 = (bf16[2,3,3,32,256]{4,3,2,1,0:T(8,128)(2,1)S(1)}, bf16[2,3,3,32,256]{4,3,2,1,0:T(8,128)(2,1)}, u32[]{:S(2)}) copy-start(bf16[2,3,3,32,256]{4,3,2,1,0:T(8,128)(2,1)} %param.16) | copy-start | bytes 884740
  0.7 1.3 %copy-start.7 = (f32[2,32]{1,0:T(2,128)S(1)}, f32[2,32]{1,0:T(2,128)}, u32[]{:S(2)}) copy-start(f32[2,32]{1,0:T(2,128)} %gb_ref.1) | copy-start | bytes 772
  0.7 1.3 %copy-start.5 = (bf16[32,8,2,16]{0,3,2,1:T(8,128)(2,1)S(1)}, bf16[32,8,2,16]{0,3,2,1:T(8,128)(2,1)}, u32[]{:S(2)}) copy-start(bf16[32,8,2,16]{0,3,2,1:T(8,128)(2,1)} %param.12) | copy-start | bytes 49156
  0.7 1.3 %copy-start.4 = (bf16[32,8,2,16]{0,3,2,1:T(8,128)(2,1)S(1)}, bf16[32,8,2,16]{0,3,2,1:T(8,128)(2,1)}, u32[]{:S(2)}) copy-start(bf16[32,8,2,16]{0,3,2,1:T(8,128)(2,1)} %param.11) | copy-start | bytes 49156
  2.1 89.8 %copy-start.1 = (bf16[128,128]{1,0:T(8,128)(2,1)S(1)}, bf16[128,128]{1,0:T(8,128)(2,1)}, u32[]{:S(2)}) copy-start(bf16[128,128]{1,0:T(8,128)(2,1)} %constant.8.clone.pm_ref) | copy-start | bytes 98308

commit v3 on v2

--- a/solution.py
+++ b/solution.py
@@ -8,7 +8,7 @@
 
 XN, ZH, YN, ZL, CN = 4, 2, 4, 8, 2
 WEDGES = YN * ZL * CN
-COPIES = 104
+COPIES = 128
 MESH = pl.DeviceIdType.MESH
 BF = jnp.bfloat16
 F32 = jnp.float32
@@ -69,11 +69,12 @@
 def kernel(
     reset_ref, x_ref, h_ref, ct_ref, wg_ref, wc_ref, gb_ref, cb_ref, q5_ref, pm_ref,
     field_ref, fin_a, fin_r, bias_ref,
-    f_ref, halo_l, halo_r, uf, near_l, near_r, far, hp, cp, wch, w_upd, w_res, w_cx, w_ch,
-    bz_s, bz_r, gs_r, gr_r, gs_u, gr_u, zs_r, zr_r, zs_u, zr_u, gpf, cs, cr,
+    f_ref, halo_l, halo_r, uf, near_l, near_r, far, hp, cp, wq, wch, w_upd, w_res, w_cx, w_ch,
+    bz_s, bz_r, gs_ri, gr_ri, gs_ui, gr_ui, gs_re, gr_re, gs_ue, gr_ue,
+    zs_ri, zr_ri, zs_ui, zr_ui, zs_re, zr_re, zs_ue, zr_ue, gpf, cs, cr,
     g1c, g1u, g2, ut, vt, blob_a, blob_r, core_a, mid_a, y_a, m_r,
     zs_a, zq_a, zf_a, zs_b, zq_b, zf_b, bs, br, bs2, br2,
-    send_sems, recv_sems,
+    send_sems, recv_sems, up_s, up_r, down_s, down_r,
 ):
     w = lax.axis_index("wedge")
     f = lax.axis_index("filt")
@@ -98,7 +99,7 @@
         return at_y((yy + d) % YN, core)
 
     def lpeer(d):
-        return (yy * ZL + (zl + d) % ZL) * CN + core, f
+        return (yy * ZL + (zl + d + ZL) % ZL) * CN + core, f
 
     partner = (w, fp)
     other_core = at_y(yy, 1 - core)
@@ -132,6 +133,38 @@
     bias_rows = [jnp.concatenate([v] * 4, axis=1) for v in (gb_ref[0:1, :], gb_ref[1:2, :], cb_ref[...])]
     bias_rows = jnp.where(row == 0, bias_rows[0], jnp.where(row == 1, bias_rows[1], bias_rows[2]))
     bz_s[...] = jnp.where(slot_a((8, 128)) == first_z, bias_rows, 0.0)
+    q5 = q5_ref[...]
+
+    def arrange(nat, out_ref):
+        lhs = jnp.concatenate(
+            [
+                jnp.concatenate([nat(a, e) for a in (ip + 1, ip)], axis=1)
+                for e in range(3)
+                for ip in range(2)
+            ],
+            axis=0,
+        )
+        out = dot_nt(lhs, q5).astype(BF)
+        for t in range(4):
+            out_ref[t] = out[:, t * 128:t * 128 + 128]
+
+    def both(gate):
+        def nat(a, e):
+            return jnp.concatenate([wg_ref[((s * 3 + a) * 3 + e) * 32:((s * 3 + a) * 3 + e) * 32 + 32, gate * 256:gate * 256 + 256] for s in range(2)], axis=0)
+
+        return nat
+
+    def input_only(a, e):
+        at = (a * 3 + e) * 32
+        return jnp.concatenate([wc_ref[at:at + 32, :], jnp.zeros((32, 256), BF)], axis=0)
+
+    def pair_hidden(a, e):
+        at = (a * 3 + e) * 32
+        return jnp.concatenate([wch[0, at:at + 32, :], wch[1, at:at + 32, :]], axis=0)
+
+    arrange(both(1), w_res)
+    arrange(both(0), w_upd)
+    arrange(input_only, w_cx)
     pl.semaphore_wait(barrier, len(peers))
 
     sends = []
@@ -162,71 +195,42 @@
         push(f_ref.at[:, second], far, partner),
         push(bz_s, bz_r, partner),
     ]
-    pair_w = push(wc_ref.at[pl.ds(288, 288), :], wch.at[zh], partner)
-    wch[zh] = wc_ref[288:576, :]
-    q5 = q5_ref[...]
-
-    def arrange(nat, out_ref):
-        lhs = jnp.concatenate(
-            [
-                jnp.concatenate([nat(a, e) for a in (ip + 1, ip)], axis=1)
-                for e in range(3)
-                for ip in range(2)
-            ],
-            axis=0,
-        )
-        out = dot_nt(lhs, q5).astype(BF)
-        for t in range(4):
-            out_ref[t] = out[:, t * 128:t * 128 + 128]
-
-    def both(ref, lo):
-        def nat(a, e):
-            rows = [((s * 3 + a) * 3 + e) * 32 for s in range(2)]
-            return jnp.concatenate([ref[r:r + 32, lo:lo + 256] for r in rows], axis=0)
-
-        return nat
-
-    def input_only(a, e):
-        at = (a * 3 + e) * 32
-        return jnp.concatenate([wc_ref[at:at + 32, :], jnp.zeros((32, 256), BF)], axis=0)
-
-    def pair_hidden(a, e):
-        at = (a * 3 + e) * 32
-        return jnp.concatenate([wch[0, at:at + 32, :], wch[1, at:at + 32, :]], axis=0)
-
-    arrange(both(wg_ref, 256), w_res)
-    arrange(both(wg_ref, 0), w_upd)
-    arrange(input_only, w_cx)
+    part = pl.multiple_of(288 + (m % 6) * 48, 16)
+    pair_w = push(wc_ref.at[pl.ds(part, 48), :], wq.at[m], partner)
+    def partial(lhs, gs_r, gr_r, gs_u, gr_u):
+        res, upd = [], []
+        for d in (2, 1, 3, 0):
+            t = (x + d) % XN
+            gs_r[t] = dot(lhs, w_res[t]).astype(BF)
+            if d:
+                res.append(push(gs_r.at[t], gr_r.at[d - 1], xpeer(d)))
+        for d in (2, 1, 3, 0):
+            t = (x + d) % XN
+            gs_u[t] = dot(lhs, jnp.concatenate([w_upd[t], w_cx[t]], axis=1)).astype(BF)
+            if d:
+                upd.append(push(gs_u.at[t], gr_u.at[d - 1], xpeer(d)))
+        return res, upd
+
+    def summed(gs, gr, copies, zs, zr):
+        value = gs[x].astype(F32)
+        landed(copies)
+        for d in range(3):
+            value = value + gr[d].astype(F32)
+        zs[...] = value.astype(BF)
+        return value, push(zs, zr, partner)
+
+    res_i, upd_i = partial(taps(uf, 32, 112), gs_ri, gr_ri, gs_ui, gr_ui)
+    sum_ri, zri = summed(gs_ri, gr_ri, res_i, zs_ri, zr_ri)
     landed(halo)
     uf[0:32, :] = halo_l[:, :128].astype(F32)
     uf[160:192, :] = halo_r[:, :128].astype(F32)
-
-    lhs = taps(uf, 0, 176)
-    res = []
-    for d in (2, 1, 3, 0):
-        t = (x + d) % XN
-        gs_r[t] = dot(lhs, w_res[t]).astype(BF)
-        if d:
-            res.append(push(gs_r.at[t], gr_r.at[d - 1], xpeer(d)))
-    lhs = taps(uf, 8, 160)
-    upd = []
-    for d in (2, 1, 3, 0):
-        t = (x + d) % XN
-        gs_u[t] = dot(lhs, jnp.concatenate([w_upd[t], w_cx[t]], axis=1)).astype(BF)
-        if d:
-            upd.append(push(gs_u.at[t], gr_u.at[d - 1], xpeer(d)))
-    sum_r = gs_r[x].astype(F32)
-    landed(res)
-    for d in range(3):
-        sum_r = sum_r + gr_r[d].astype(F32)
-    zs_r[...] = sum_r.astype(BF)
-    zr = push(zs_r, zr_r, partner)
-    sum_u = gs_u[x].astype(F32)
-    landed(upd)
-    for d in range(3):
-        sum_u = sum_u + gr_u[d].astype(F32)
-    zs_u[...] = sum_u.astype(BF)
-    zu = push(zs_u, zr_u, partner)
+    lhs = jnp.concatenate([taps(uf, 0, 32), taps(uf, 144, 32)], axis=0)
+    res_e, upd_e = partial(lhs, gs_re, gr_re, gs_ue, gr_ue)
+    sum_re, zre = summed(gs_re, gr_re, res_e, zs_re, zr_re)
+    sum_ui, zui = summed(gs_ui, gr_ui, upd_i, zs_ui, zr_ui)
+    sum_ue, zue = summed(gs_ue, gr_ue, upd_e, zs_ue, zr_ue)
+    pair_w.wait_recv()
+    shares = [push(wq.at[m], wq.at[m], mpeer(d)) for d in range(1, 8)]
 
     for e in range(3):
         ut[e * 128:e * 128 + 128, :] = uf[(e + 3) * 8:(e + 3) * 8 + 128, :].T.astype(BF)
@@ -241,11 +245,18 @@
         at = slot_a(mine.shape)
         hp[lo:lo + mine.shape[0], :] = jnp.where(at, swap(block_0), block_1)
         cp[lo:lo + mine.shape[0], :] = jnp.where(at, block_0, swap(block_1))
-    pair_w.wait_recv()
+    landed(shares)
+    wch[zh] = wc_ref[288:576, :]
+    for k in range(6):
+        wch[1 - zh, k * 48:k * 48 + 48, :] = wq[k]
     arrange(pair_hidden, w_ch)
 
-    zr.wait_recv()
-    r = jax.nn.sigmoid(sum_r + zr_r[...].astype(F32) + biases[1:2, :])
+    def joined(edge, inner):
+        return jnp.concatenate([edge[:32], inner, edge[32:]], axis=0)
+
+    landed([zri, zre])
+    sum_r = joined(sum_re + zr_re[...].astype(F32), sum_ri + zr_ri[...].astype(F32))
+    r = jax.nn.sigmoid(sum_r + biases[1:2, :])
     gp = (r * hp[8:184, :]).astype(BF).astype(F32)
     gpf[...] = gp
 
@@ -259,8 +270,8 @@
     own_v = jnp.where(slot_a((176, 128)), uf[8:184, :], own_b(gp))
     for e in range(3):
         vt[e * 128:e * 128 + 128, :] = own_v[(e + 2) * 8:(e + 2) * 8 + 128].T.astype(BF)
-    zu.wait_recv()
-    sum_u = sum_u + zr_u[...].astype(F32)
+    landed([zui, zue])
+    sum_u = joined(sum_ue + zr_ue[...].astype(F32), sum_ui + zr_ui[...].astype(F32))[8:168]
     u = jax.nn.sigmoid(sum_u[:, :128] + biases[0:1, :])
     pre = sum_u[:, 128:] + biases[2:3, :] + cs[x].astype(F32)
     landed(cand)
@@ -332,15 +343,59 @@
     hidden = own_b(direct + gg[8:136] * r[24:152])
     field_ref[:, 128:] = jnp.where(slot_a((128, 128)), total, hidden + total).astype(BF)
 
+    def reduce_z(owners, mine, came, out, which):
+        def copy(src, dst, send, recv, z):
+            return pltpu.make_async_remote_copy(
+                src_ref=src, dst_ref=dst, send_sem=send, recv_sem=recv, device_id=lpeer(z - zl), device_id_type=MESH
+            )
+
+        def up(i, s, p):
+            return copy(mine.at[i], came.at[s], up_s.at[which, i], up_r.at[which, s], p)
+
+        def down(i, d, z):
+            return copy(out.at[i], out.at[i], down_s.at[which, d - 1], down_r.at[which, i], z)
+
+        for i, p in enumerate(owners):
+            pl.when(zl != p)(up(i, zl, p).start)
+
+        def own():
+            for i, p in enumerate(owners):
+                @pl.when(zl == p)
+                def _():
+                    value = mine[i].astype(F32)
+                    for s in range(8):
+                        if s != p:
+                            up(i, s, p).wait_recv()
+                            value = value + came[s].astype(F32)
+                    out[i] = value.astype(BF)
+                    for d in range(1, 8):
+                        down(i, d, (p + d) % 8).start()
+
+        def back():
+            for i, p in enumerate(owners):
+                pl.when(zl != p)(down(i, 1, p).wait_recv)
+
+        def close():
+            for i, p in enumerate(owners):
+                @pl.when(zl != p)
+                def _():
+                    up(i, zl, p).wait_send()
+
+                @pl.when(zl == p)
+                def _():
+                    for d in range(1, 8):
+                        down(i, d, (p + d) % 8).wait_send()
+
+        return own, back, close
+
     acc = mid_a[yy].astype(F32)
     landed(over_y)
     for d in range(3):
         acc = acc + y_a[d].astype(F32)
-    for p in range(6):
-        zs_a[p] = acc[p * 48:p * 48 + 48].astype(BF)
-    for p in (6, 7):
-        zs_a[p] = jnp.zeros((48, 128), BF)
-    over_za = [push(zs_a.at[(zl + d) % ZL], zq_a.at[d - 1], lpeer(d)) for d in range(1, 8)]
+    for p in range(3):
+        zs_a[p] = acc[p * 80:p * 80 + 80].astype(BF)
+    zs_a[3] = jnp.concatenate([acc[240:288], jnp.zeros((32, 128), F32)], axis=0).astype(BF)
+    own_za, back_za, close_za = reduce_z((2, 3, 4, 5), zs_a, zq_a, zf_a, 0)
     b1 = bs[...]
     landed(bias1)
     for d in range(7):
@@ -351,23 +406,11 @@
     landed(over_m)
     for d in range(7):
         acc = acc + m_r[d].astype(F32)
-    for p in range(4):
-        zs_b[p] = acc[p * 32:p * 32 + 32].astype(BF)
-    zs_b[4] = jnp.concatenate([acc[128:144], jnp.zeros((16, 128), F32)], axis=0).astype(BF)
-    for p in (5, 6, 7):
-        zs_b[p] = jnp.zeros((32, 128), BF)
-    over_zb = [push(zs_b.at[(zl + d) % ZL], zq_b.at[d - 1], lpeer(d)) for d in range(1, 8)]
-
-    def own_sum(mine, came, copies, out):
-        value = mine[zl].astype(F32)
-        landed(copies)
-        for d in range(7):
-            value = value + came[d].astype(F32)
-        out[zl] = value.astype(BF)
-        return [push(out.at[zl], out.at[zl], lpeer(d)) for d in range(1, 8)]
-
-    back_a = own_sum(zs_a, zq_a, over_za, zf_a)
-    back_b = own_sum(zs_b, zq_b, over_zb, zf_b)
+    zs_b[0] = acc[0:80].astype(BF)
+    zs_b[1] = jnp.concatenate([acc[80:144], jnp.zeros((16, 128), F32)], axis=0).astype(BF)
+    own_zb, back_zb, close_zb = reduce_z((3, 4), zs_b, zq_b, zf_b, 1)
+    own_za()
+    own_zb()
 
     def spread(fin):
         to_y = [push(fin.at[m], fin.at[m], ypeer(d)) for d in (2, 1, 3)]
@@ -379,14 +422,14 @@
             at = ((yy + YN - d) % YN) * CN + core
             rest.append(push(fin.at[at], fin.at[at], other_core))
 
-    landed(back_a)
-    for p in range(6):
-        fin_a[m, p * 48:p * 48 + 48, :] = zf_a[p]
+    back_za()
+    for p in range(3):
+        fin_a[m, p * 80:p * 80 + 80, :] = zf_a[p]
+    fin_a[m, 240:288, :] = zf_a[3, 0:48, :]
     to_ya, rest_a = spread(fin_a)
-    landed(back_b)
-    for p in range(4):
-        fin_r[m, p * 32:p * 32 + 32, :] = zf_b[p]
-    fin_r[m, 128:144, :] = zf_b[4, 0:16, :]
+    back_zb()
+    fin_r[m, 0:80, :] = zf_b[0]
+    fin_r[m, 80:144, :] = zf_b[1, 0:64, :]
     to_yr, rest_r = spread(fin_r)
     b2 = bs2[...]
     landed(bias2)
@@ -397,6 +440,8 @@
     forward(fin_r, to_yr, rest_r)
     landed(rest_a)
     landed(rest_r)
+    close_za()
+    close_zb()
     for copy in sends:
         copy.wait_send()
 
@@ -461,15 +506,19 @@
 
     scratch = [
         bf(128, 256), bf(32, 256), bf(32, 256), f32(192, 128), bf(32, 128), bf(32, 128), bf(128, 128),
-        f32(192, 128), f32(192, 128), bf(2, 288, 256),
+        f32(192, 128), f32(192, 128), bf(8, 48, 256), bf(2, 288, 256),
         bf(4, 384, 128), bf(4, 384, 128), bf(4, 384, 128), bf(4, 384, 128),
-        f32(8, 128), f32(8, 128), bf(4, 176, 128), bf(3, 176, 128), bf(4, 160, 256), bf(3, 160, 256),
-        bf(176, 128), bf(176, 128), bf(160, 256), bf(160, 256), f32(176, 128), bf(4, 160, 128), bf(3, 160, 128),
+        f32(8, 128), f32(8, 128), bf(4, 112, 128), bf(3, 112, 128), bf(4, 112, 256), bf(3, 112, 256),
+        bf(4, 64, 128), bf(3, 64, 128), bf(4, 64, 256), bf(3, 64, 256),
+        bf(112, 128), bf(112, 128), bf(112, 256), bf(112, 256), bf(64, 128), bf(64, 128), bf(64, 256), bf(64, 256),
+        f32(176, 128), bf(4, 160, 128), bf(3, 160, 128),
         bf(4, 160, 128), bf(4, 160, 128), bf(4, 160, 128), bf(384, 128), bf(384, 128),
         bf(2304, 128), bf(1152, 128), bf(4, 288, 128), bf(4, 288, 128), bf(3, 288, 128), bf(7, 144, 128),
-        bf(8, 48, 128), bf(7, 48, 128), bf(8, 48, 128), bf(8, 32, 128), bf(7, 32, 128), bf(8, 32, 128),
+        bf(4, 80, 128), bf(8, 80, 128), bf(4, 80, 128), bf(2, 80, 128), bf(8, 80, 128), bf(2, 80, 128),
         f32(8, 128), f32(7, 8, 128), f32(8, 128), f32(7, 8, 128),
         pltpu.SemaphoreType.DMA((COPIES,)), pltpu.SemaphoreType.DMA((COPIES,)),
+        pltpu.SemaphoreType.DMA((2, 4)), pltpu.SemaphoreType.DMA((2, 8)),
+        pltpu.SemaphoreType.DMA((2, 7)), pltpu.SemaphoreType.DMA((2, 4)),
     ]
     q5 = jnp.asarray(block_transpose(4, 2, 64), BF)
     rows_in = jnp.asarray(row_order(), BF)

time: 94.5 us -> 85.6 us (0.906)
  Pallas kernels: 92.2 us -> 83.3 us
    pallas_call x1, Pallas kernels: 89.8 us -> 80.9 us  [per_device(): pl.pallas_call(kernel, out_shape=(jax.ShapeDtypeStruct((128, 256), BF), j...]
where the time goes in v3:
time: 85.6 us; the launch traced here: 85.4 us
  Pallas kernels  83.3 us (97%)
  local copies, waits for them, and re-layouts  1.28 us (1%)
    pallas_call x1, Pallas kernels, per_device(): pl.pallas_call(kernel, out_shape=(jax.ShapeDtypeStruct((128, 256), BF), j...  80.9 us
    pallas_call x1, Pallas kernels, per_device(): pl.pallas_call(finish, out_shape=(shape, shape, shape, jax.ShapeDtypeStru...  2.43 us

profile of v3, /device:TPU:1, one launch (start us, length us, event | category | flops | bytes accessed | tf_op | source)
XLA Modules:
  0.0 85.4 jit_solution(16151362511674003323)
XLA Ops:
  0.6 0.0 copy-start
  0.6 0.0 copy-start.9
  0.7 0.0 copy-start.2
  0.7 0.0 copy-start.6
  0.7 0.0 copy-start.8
  0.7 0.0 copy-start.3
  0.7 0.0 copy-start.7
  0.7 0.0 copy-start.5
  0.7 0.0 copy-start.4
  0.7 1.2 %copy.18 = bf16[72,8,2,256]{3,1,2,0:T(8,128)(2,1)S(1)} copy(bf16[72,8,2,256]{3,2,1,0:T(2,128)(2,1)} %bitcast.18) | data formatting | bytes 1179648
  2.0 0.0 copy-done
  2.0 0.0 copy-done.9
  2.0 0.0 copy-done.2
  2.0 0.0 copy-done.6
  2.0 0.0 copy-done.8
  2.0 0.0 copy-done.3
  2.0 0.0 copy-done.7
  2.0 0.0 copy-done.5
  2.0 0.0 copy-done.4
  2.1 0.0 copy-start.1
  2.1 80.9 %shard_map.162 = (bf16[128,256]{1,0:T(8,128)(2,1)S(1)}, bf16[8,288,128]{2,1,0:T(8,128)(2,1)S(1)}, bf16[8,144,128]{2,1,0:T(8,128)(2,1)S(1)}, f32[8,128]{1,0:T(8,128)S(1)}) custom-call(s32[8]{0:T(128)S(1)} %copy-done.2, bf16[8,2,16,32]{3,2,1,0:T(8,128)(2,1)S(1)} %bitcast.14, bf16[8,2,16,32]{3,2,1,0:T(8,128)(2,1)S(1)} %bitcast.15, ...), custom_call_target="tpu_custom_call" | custom-call | flops 1000000000 | bytes 8000000 | tf_op jit(solution)/shard_map/pallas_call | solution.py:529
  82.9 0.0 copy-done.1
  82.9 2.4 %shard_map.163 = (bf16[8,2,16,32]{3,2,1,0:T(8,128)(2,1)}, bf16[8,2,16,32]{3,2,1,0:T(8,128)(2,1)}, bf16[8,2,16,32]{3,2,1,0:T(8,128)(2,1)}, f32[2,3,3,32,2,256]{5,...) custom-call(s32[8]{0:T(128)S(1)} %copy-done.2, ...), custom_call_target="tpu_custom_call" | custom-call | tf_op jit(solution)/shard_map/pallas_call | solution.py:549
Async XLA Ops:
  0.6 1.3 %copy-start = (bf16[512,512]{1,0:T(8,128)(2,1)S(1)}, bf16[512,512]{1,0:T(8,128)(2,1)}, u32[]{:S(2)}) copy-start(bf16[512,512]{1,0:T(8,128)(2,1)} %constant.6.clone.q5_ref) | copy-start | bytes 1572868
  0.6 1.3 %copy-start.9 = (bf16[128,128]{1,0:T(8,128)(2,1)S(1)}, bf16[128,128]{1,0:T(8,128)(2,1)}, u32[]{:S(2)}) copy-start(bf16[128,128]{1,0:T(8,128)(2,1)} %constant.7.clone.pm_ref) | copy-start | bytes 98308
  0.7 1.3 %copy-start.2 = (s32[8]{0:T(128)S(1)}, s32[8]{0:T(128)}, u32[]{:S(2)}) copy-start(s32[8]{0:T(128)} %reset_ref.3) | copy-start | bytes 100
  0.7 1.3 %copy-start.6 = (bf16[32,8,2,16]{0,3,2,1:T(8,128)(2,1)S(1)}, bf16[32,8,2,16]{0,3,2,1:T(8,128)(2,1)}, u32[]{:S(2)}) copy-start(bf16[32,8,2,16]{0,3,2,1:T(8,128)(2,1)} %param.18) | copy-start | bytes 49156
  0.7 1.3 %copy-start.8 = (f32[32]{0:T(128)S(1)}, f32[32]{0:T(128)}, u32[]{:S(2)}) copy-start(f32[32]{0:T(128)} %param.17) | copy-start | bytes 388
  0.7 1.3 %copy-start.3 = (bf16[2,3,3,32,256]{4,3,2,1,0:T(8,128)(2,1)S(1)}, bf16[2,3,3,32,256]{4,3,2,1,0:T(8,128)(2,1)}, u32[]{:S(2)}) copy-start(bf16[2,3,3,32,256]{4,3,2,1,0:T(8,128)(2,1)} %param.16) | copy-start | bytes 884740
  0.7 1.3 %copy-start.7 = (f32[2,32]{1,0:T(2,128)S(1)}, f32[2,32]{1,0:T(2,128)}, u32[]{:S(2)}) copy-start(f32[2,32]{1,0:T(2,128)} %gb_ref.1) | copy-start | bytes 772
  0.7 1.3 %copy-start.5 = (bf16[32,8,2,16]{0,3,2,1:T(8,128)(2,1)S(1)}, bf16[32,8,2,16]{0,3,2,1:T(8,128)(2,1)}, u32[]{:S(2)}) copy-start(bf16[32,8,2,16]{0,3,2,1:T(8,128)(2,1)} %param.12) | copy-start | bytes 49156
  0.7 1.3 %copy-start.4 = (bf16[32,8,2,16]{0,3,2,1:T(8,128)(2,1)S(1)}, bf16[32,8,2,16]{0,3,2,1:T(8,128)(2,1)}, u32[]{:S(2)}) copy-start(bf16[32,8,2,16]{0,3,2,1:T(8,128)(2,1)} %param.11) | copy-start | bytes 49156
  2.1 80.9 %copy-start.1 = (bf16[128,128]{1,0:T(8,128)(2,1)S(1)}, bf16[128,128]{1,0:T(8,128)(2,1)}, u32[]{:S(2)}) copy-start(bf16[128,128]{1,0:T(8,128)(2,1)} %constant.8.clone.pm_ref) | copy-start | bytes 98308

commit v4 on v3

--- a/solution.py
+++ b/solution.py
@@ -8,7 +8,7 @@
 
 XN, ZH, YN, ZL, CN = 4, 2, 4, 8, 2
 WEDGES = YN * ZL * CN
-COPIES = 128
+COPIES = 112
 MESH = pl.DeviceIdType.MESH
 BF = jnp.bfloat16
 F32 = jnp.float32
@@ -306,7 +306,7 @@
 
     low = lax.broadcasted_iota(jnp.int32, (64, 128), 1) < 64
 
-    def weight_grad(left_ref, grad_ref, out_ref, start):
+    def weight_grad(left_ref, grad_ref, place):
         left_rows = left_ref[...]
         for q in range(2):
             rhs = jnp.concatenate([grad_ref[2 * q, 16:144, :], grad_ref[2 * q + 1, 16:144, :]], axis=1)
@@ -320,25 +320,24 @@
                     jnp.where(low, t0[:64] + roll(t0[64:], 64), t1[64:] + roll(t1[:64], 64)),
                 )
                 for k, slab in enumerate(slabs):
-                    n = (start + e * 6 + q * 3 + k) * 64
-                    out_ref[n:n + 64, :] = slab.astype(BF)
+                    out_ref, n = place(e, q * 3 + k)
+                    out_ref[n * 64:n * 64 + 64, :] = slab.astype(BF)
 
     def chunk(t, rows):
         return pl.ds(pl.multiple_of(t * rows, 16), rows)
 
-    weight_grad(vt, g1c, blob_a, 0)
+    weight_grad(vt, g1c, lambda e, k: (blob_a, e * 6 + k))
     landed(got_u)
-    weight_grad(ut, g1u, blob_a, 18)
-    half = [push(blob_a.at[chunk(t * CN + 1 - core, 288), :], core_a.at[t], other_core) for t in range(4)]
+    weight_grad(ut, g1u, lambda e, k: (blob_a, 18 + e * 6 + k) if e < 2 else (blob_r, 18 + k))
+    half = [push(blob_a.at[chunk(t * CN + 1 - core, 240), :], core_a.at[t], other_core) for t in range(4)]
     total = shifted(dot_nt(grads, tiles(w_cx)), 8, 128) + shifted(dot_nt(tiles(g1u), tiles(w_upd)), 8, 128)
+    landed(got_r)
+    weight_grad(ut, g2, lambda e, k: (blob_r, e * 6 + k))
+    over_m = [push(blob_r.at[chunk((m + d) % 8, 192), :], m_r.at[d - 1], mpeer(d)) for d in range(1, 8)]
     landed(half)
     for t in range(4):
-        mid_a[t] = (blob_a[chunk(t * CN + core, 288), :].astype(F32) + core_a[t].astype(F32)).astype(BF)
+        mid_a[t] = (blob_a[chunk(t * CN + core, 240), :].astype(F32) + core_a[t].astype(F32)).astype(BF)
     over_y = [push(mid_a.at[(yy + d) % YN], y_a.at[d - 1], ypeer(d)) for d in (2, 1, 3)]
-
-    landed(got_r)
-    weight_grad(ut, g2, blob_r, 0)
-    over_m = [push(blob_r.at[chunk((m + d) % 8, 144), :], m_r.at[d - 1], mpeer(d)) for d in range(1, 8)]
     total = total + shifted(dot_nt(tiles(g2), tiles(w_res)), 8, 128)
     hidden = own_b(direct + gg[8:136] * r[24:152])
     field_ref[:, 128:] = jnp.where(slot_a((128, 128)), total, hidden + total).astype(BF)
@@ -394,20 +393,19 @@
         acc = acc + y_a[d].astype(F32)
     for p in range(3):
         zs_a[p] = acc[p * 80:p * 80 + 80].astype(BF)
-    zs_a[3] = jnp.concatenate([acc[240:288], jnp.zeros((32, 128), F32)], axis=0).astype(BF)
-    own_za, back_za, close_za = reduce_z((2, 3, 4, 5), zs_a, zq_a, zf_a, 0)
+    own_za, back_za, close_za = reduce_z((2, 3, 4), zs_a, zq_a, zf_a, 0)
     b1 = bs[...]
     landed(bias1)
     for d in range(7):
         b1 = b1 + br[d]
     bs2[...] = b1
     bias2 = [push(bs2, br2.at[d - 1], lpeer(d)) for d in range(1, 8)]
-    acc = blob_r[chunk(m, 144), :].astype(F32)
+    acc = blob_r[chunk(m, 192), :].astype(F32)
     landed(over_m)
     for d in range(7):
         acc = acc + m_r[d].astype(F32)
-    zs_b[0] = acc[0:80].astype(BF)
-    zs_b[1] = jnp.concatenate([acc[80:144], jnp.zeros((16, 128), F32)], axis=0).astype(BF)
+    for p in range(2):
+        zs_b[p] = acc[p * 96:p * 96 + 96].astype(BF)
     own_zb, back_zb, close_zb = reduce_z((3, 4), zs_b, zq_b, zf_b, 1)
     own_za()
     own_zb()
@@ -425,19 +423,18 @@
     back_za()
     for p in range(3):
         fin_a[m, p * 80:p * 80 + 80, :] = zf_a[p]
-    fin_a[m, 240:288, :] = zf_a[3, 0:48, :]
     to_ya, rest_a = spread(fin_a)
     back_zb()
-    fin_r[m, 0:80, :] = zf_b[0]
-    fin_r[m, 80:144, :] = zf_b[1, 0:64, :]
+    for p in range(2):
+        fin_r[m, p * 96:p * 96 + 96, :] = zf_b[p]
     to_yr, rest_r = spread(fin_r)
     b2 = bs2[...]
     landed(bias2)
     for d in range(7):
         b2 = b2 + br2[d]
     bias_ref[...] = own_a(b2)
+    forward(fin_r, to_yr, rest_r)
     forward(fin_a, to_ya, rest_a)
-    forward(fin_r, to_yr, rest_r)
     landed(rest_a)
     landed(rest_r)
     close_za()
@@ -462,9 +459,12 @@
     gb_ref[...] = sums[0:2, 0:32]
     cb_ref[...] = sums[2:3, 0:32]
 
-    def slab(fin, size, step, n):
-        pieces = [fin[r // size, r % size:r % size + step, :] for r in range(n * 64, n * 64 + 64, step)]
+    def slab_a(n):
+        pieces = [fin_a[r // 240, r % 240:r % 240 + 16, :] for r in range(n * 64, n * 64 + 64, 16)]
         return jnp.concatenate(pieces, axis=0)
+
+    def slab_r(n):
+        return fin_r[n // 3, n % 3 * 64:n % 3 * 64 + 64, :]
 
     def put(gate, a, e, value):
         for s in range(2):
@@ -475,11 +475,14 @@
                 wgg_ref[s, a, e, :, gate, :] = part
 
     q5 = q5_ref[...]
-    for gate, fin, size, step, start in (
-        (None, fin_a, 288, 32, 0), (0, fin_a, 288, 32, 18), (1, fin_r, 144, 16, 0)
-    ):
+    for gate in (None, 0, 1):
         def get(e, q, k):
-            return slab(fin, size, step, start + e * 6 + q * 3 + k)
+            n = e * 6 + q * 3 + k
+            if gate is None:
+                return slab_a(n)
+            if gate == 1:
+                return slab_r(n)
+            return slab_a(18 + n) if e < 2 else slab_r(6 + n)
 
         outer = jnp.concatenate(
             [
@@ -513,8 +516,8 @@
         bf(112, 128), bf(112, 128), bf(112, 256), bf(112, 256), bf(64, 128), bf(64, 128), bf(64, 256), bf(64, 256),
         f32(176, 128), bf(4, 160, 128), bf(3, 160, 128),
         bf(4, 160, 128), bf(4, 160, 128), bf(4, 160, 128), bf(384, 128), bf(384, 128),
-        bf(2304, 128), bf(1152, 128), bf(4, 288, 128), bf(4, 288, 128), bf(3, 288, 128), bf(7, 144, 128),
-        bf(4, 80, 128), bf(8, 80, 128), bf(4, 80, 128), bf(2, 80, 128), bf(8, 80, 128), bf(2, 80, 128),
+        bf(1920, 128), bf(1536, 128), bf(4, 240, 128), bf(4, 240, 128), bf(3, 240, 128), bf(7, 192, 128),
+        bf(3, 80, 128), bf(8, 80, 128), bf(3, 80, 128), bf(2, 96, 128), bf(8, 96, 128), bf(2, 96, 128),
         f32(8, 128), f32(7, 8, 128), f32(8, 128), f32(7, 8, 128),
         pltpu.SemaphoreType.DMA((COPIES,)), pltpu.SemaphoreType.DMA((COPIES,)),
         pltpu.SemaphoreType.DMA((2, 4)), pltpu.SemaphoreType.DMA((2, 8)),
@@ -530,8 +533,8 @@
         kernel,
         out_shape=(
             jax.ShapeDtypeStruct((128, 256), BF),
-            jax.ShapeDtypeStruct((8, 288, 128), BF),
-            jax.ShapeDtypeStruct((8, 144, 128), BF),
+            jax.ShapeDtypeStruct((8, 240, 128), BF),
+            jax.ShapeDtypeStruct((8, 192, 128), BF),
             jax.ShapeDtypeStruct((8, 128), F32),
         ),
         in_specs=[smem] + [whole] * 9,

time: 85.6 us -> 84.1 us (0.982)
  Pallas kernels: 83.3 us -> 81.8 us
    pallas_call x1, Pallas kernels: 80.9 us -> 79.4 us  [per_device(): pl.pallas_call(kernel, out_shape=(jax.ShapeDtypeStruct((128, 256), BF), j...]
where the time goes in v4:
time: 84.1 us; the launch traced here: 83.9 us
  Pallas kernels  81.8 us (97%)
  local copies, waits for them, and re-layouts  1.28 us (2%)
    pallas_call x1, Pallas kernels, per_device(): pl.pallas_call(kernel, out_shape=(jax.ShapeDtypeStruct((128, 256), BF), j...  79.4 us
    pallas_call x1, Pallas kernels, per_device(): pl.pallas_call(finish, out_shape=(shape, shape, shape, jax.ShapeDtypeStru...  2.43 us

profile of v4, /device:TPU:1, one launch (start us, length us, event | category | flops | bytes accessed | tf_op | source)
XLA Modules:
  0.0 83.9 jit_solution(6850183856189161654)
XLA Ops:
  0.6 0.0 copy-start
  0.6 0.0 copy-start.9
  0.7 0.0 copy-start.2
  0.7 0.0 copy-start.6
  0.7 0.0 copy-start.8
  0.7 0.0 copy-start.3
  0.7 0.0 copy-start.7
  0.7 0.0 copy-start.5
  0.7 0.0 copy-start.4
  0.7 1.2 %copy.18 = bf16[72,8,2,256]{3,1,2,0:T(8,128)(2,1)S(1)} copy(bf16[72,8,2,256]{3,2,1,0:T(2,128)(2,1)} %bitcast.18) | data formatting | bytes 1179648
  2.0 0.0 copy-done
  2.0 0.0 copy-done.9
  2.0 0.0 copy-done.2
  2.0 0.0 copy-done.6
  2.0 0.0 copy-done.8
  2.0 0.0 copy-done.3
  2.0 0.0 copy-done.7
  2.0 0.0 copy-done.5
  2.0 0.0 copy-done.4
  2.1 0.0 copy-start.1
  2.1 79.4 %shard_map.162 = (bf16[128,256]{1,0:T(8,128)(2,1)S(1)}, bf16[8,240,128]{2,1,0:T(8,128)(2,1)S(1)}, bf16[8,192,128]{2,1,0:T(8,128)(2,1)S(1)}, f32[8,128]{1,0:T(8,128)S(1)}) custom-call(s32[8]{0:T(128)S(1)} %copy-done.2, bf16[8,2,16,32]{3,2,1,0:T(8,128)(2,1)S(1)} %bitcast.14, bf16[8,2,16,32]{3,2,1,0:T(8,128)(2,1)S(1)} %bitcast.15, ...), custom_call_target="tpu_custom_call" | custom-call | flops 1000000000 | bytes 8000000 | tf_op jit(solution)/shard_map/pallas_call | solution.py:532
  81.4 0.0 copy-done.1
  81.5 2.4 %shard_map.163 = (bf16[8,2,16,32]{3,2,1,0:T(8,128)(2,1)}, bf16[8,2,16,32]{3,2,1,0:T(8,128)(2,1)}, bf16[8,2,16,32]{3,2,1,0:T(8,128)(2,1)}, f32[2,3,3,32,2,256]{5,...) custom-call(s32[8]{0:T(128)S(1)} %copy-done.2, ...), custom_call_target="tpu_custom_call" | custom-call | tf_op jit(solution)/shard_map/pallas_call | solution.py:552
Async XLA Ops:
  0.6 1.3 %copy-start = (bf16[512,512]{1,0:T(8,128)(2,1)S(1)}, bf16[512,512]{1,0:T(8,128)(2,1)}, u32[]{:S(2)}) copy-start(bf16[512,512]{1,0:T(8,128)(2,1)} %constant.6.clone.q5_ref) | copy-start | bytes 1572868
  0.6 1.3 %copy-start.9 = (bf16[128,128]{1,0:T(8,128)(2,1)S(1)}, bf16[128,128]{1,0:T(8,128)(2,1)}, u32[]{:S(2)}) copy-start(bf16[128,128]{1,0:T(8,128)(2,1)} %constant.7.clone.pm_ref) | copy-start | bytes 98308
  0.7 1.3 %copy-start.2 = (s32[8]{0:T(128)S(1)}, s32[8]{0:T(128)}, u32[]{:S(2)}) copy-start(s32[8]{0:T(128)} %reset_ref.3) | copy-start | bytes 100
  0.7 1.3 %copy-start.6 = (bf16[32,8,2,16]{0,3,2,1:T(8,128)(2,1)S(1)}, bf16[32,8,2,16]{0,3,2,1:T(8,128)(2,1)}, u32[]{:S(2)}) copy-start(bf16[32,8,2,16]{0,3,2,1:T(8,128)(2,1)} %param.18) | copy-start | bytes 49156
  0.7 1.3 %copy-start.8 = (f32[32]{0:T(128)S(1)}, f32[32]{0:T(128)}, u32[]{:S(2)}) copy-start(f32[32]{0:T(128)} %param.17) | copy-start | bytes 388
  0.7 1.3 %copy-start.3 = (bf16[2,3,3,32,256]{4,3,2,1,0:T(8,128)(2,1)S(1)}, bf16[2,3,3,32,256]{4,3,2,1,0:T(8,128)(2,1)}, u32[]{:S(2)}) copy-start(bf16[2,3,3,32,256]{4,3,2,1,0:T(8,128)(2,1)} %param.16) | copy-start | bytes 884740
  0.7 1.3 %copy-start.7 = (f32[2,32]{1,0:T(2,128)S(1)}, f32[2,32]{1,0:T(2,128)}, u32[]{:S(2)}) copy-start(f32[2,32]{1,0:T(2,128)} %gb_ref.1) | copy-start | bytes 772
  0.7 1.3 %copy-start.5 = (bf16[32,8,2,16]{0,3,2,1:T(8,128)(2,1)S(1)}, bf16[32,8,2,16]{0,3,2,1:T(8,128)(2,1)}, u32[]{:S(2)}) copy-start(bf16[32,8,2,16]{0,3,2,1:T(8,128)(2,1)} %param.12) | copy-start | bytes 49156
  0.7 1.3 %copy-start.4 = (bf16[32,8,2,16]{0,3,2,1:T(8,128)(2,1)S(1)}, bf16[32,8,2,16]{0,3,2,1:T(8,128)(2,1)}, u32[]{:S(2)}) copy-start(bf16[32,8,2,16]{0,3,2,1:T(8,128)(2,1)} %param.11) | copy-start | bytes 49156
  2.1 79.4 %copy-start.1 = (bf16[128,128]{1,0:T(8,128)(2,1)S(1)}, bf16[128,128]{1,0:T(8,128)(2,1)}, u32[]{:S(2)}) copy-start(bf16[128,128]{1,0:T(8,128)(2,1)} %constant.8.clone.pm_ref) | copy-start | bytes 98308

commit v5 on v4

--- a/solution.py
+++ b/solution.py
@@ -445,20 +445,9 @@
 
 def finish(
     reset_ref, field_ref, fin_a, fin_r, bias_ref, q5_ref, pm_ref,
-    hn_ref, gx_ref, gh_ref, wgg_ref, gb_ref, wgc_ref, cb_ref,
+    hn_ref, gx_ref, gh_ref, wgg_out, gb_ref, wgc_out, cb_ref,
+    wgg_ref, wgc_ref, sems,
 ):
-    rows = dot(pm_ref[...], field_ref[...])
-    for i in range(2):
-        hn_ref[:, i] = rows[:, i * 64:i * 64 + 32].reshape(8, 16, 32).astype(BF)
-        gx_ref[:, i] = rows[:, 128 + i * 64:160 + i * 64].reshape(8, 16, 32).astype(BF)
-        value = rows[:, 160 + i * 64:192 + i * 64].reshape(8, 16, 32)
-        for b in range(8):
-            gh_ref[b, i] = (value[b] * (1 - reset_ref[b]).astype(F32)).astype(BF)
-    sums = bias_ref[...]
-    sums = sums + roll(sums, 64)
-    gb_ref[...] = sums[0:2, 0:32]
-    cb_ref[...] = sums[2:3, 0:32]
-
     def slab_a(n):
         pieces = [fin_a[r // 240, r % 240:r % 240 + 16, :] for r in range(n * 64, n * 64 + 64, 16)]
         return jnp.concatenate(pieces, axis=0)
@@ -472,8 +461,9 @@
             if gate is None:
                 wgc_ref[s, a, e] = part
             else:
-                wgg_ref[s, a, e, :, gate, :] = part
-
+                later[s].append((a, e, gate, part))
+
+    later = ([], [])
     q5 = q5_ref[...]
     for gate in (None, 0, 1):
         def get(e, q, k):
@@ -498,6 +488,28 @@
             put(gate, 0, e, outer[at, 256:])
             inner = jnp.concatenate([get(e, q, 2) for q in range(2)], axis=1)
             put(gate, 1, e, inner.astype(F32))
+        if gate is None:
+            copies = [pltpu.make_async_copy(wgc_ref, wgc_out, sems.at[0])]
+            copies[0].start()
+    for s in range(2):
+        for a, e, gate, part in later[s]:
+            wgg_ref[s, a, e, :, gate, :] = part
+        copies.append(pltpu.make_async_copy(wgg_ref.at[s], wgg_out.at[s], sems.at[1 + s]))
+        copies[-1].start()
+
+    rows = dot(pm_ref[...], field_ref[...])
+    for i in range(2):
+        hn_ref[:, i] = rows[:, i * 64:i * 64 + 32].reshape(8, 16, 32).astype(BF)
+        gx_ref[:, i] = rows[:, 128 + i * 64:160 + i * 64].reshape(8, 16, 32).astype(BF)
+        value = rows[:, 160 + i * 64:192 + i * 64].reshape(8, 16, 32)
+        for b in range(8):
+            gh_ref[b, i] = (value[b] * (1 - reset_ref[b]).astype(F32)).astype(BF)
+    sums = bias_ref[...]
+    sums = sums + roll(sums, 64)
+    gb_ref[...] = sums[0:2, 0:32]
+    cb_ref[...] = sums[2:3, 0:32]
+    for copy in copies:
+        copy.wait()
 
 
 def per_device(x_in, h_prev, reset, w_gate, gate_bias, w_cand, cand_bias, cotangent):
@@ -557,7 +569,8 @@
             jax.ShapeDtypeStruct(w_cand.shape, F32), jax.ShapeDtypeStruct((1, 32), F32),
         ),
         in_specs=[smem] + [whole] * 6,
-        out_specs=[whole] * 7,
+        out_specs=[whole, whole, whole, pl.BlockSpec(memory_space=pl.ANY), whole, pl.BlockSpec(memory_space=pl.ANY), whole],
+        scratch_shapes=[f32(*w_gate.shape), f32(*w_cand.shape), pltpu.SemaphoreType.DMA((3,))],
         compiler_params=pltpu.CompilerParams(vmem_limit_bytes=32 * 1024 * 1024),
     )(reset, field, fin_a, fin_r, bias, q5, rows_out)
     back = lambda v: v.transpose(3, 0, 1, 2)

time: 84.1 us -> 84.6 us (level)
  no operation moved by 1% of the time
where the time goes in v5:
time: 84.6 us; the launch traced here: 84.5 us
  Pallas kernels  82.4 us (97%)
  local copies, waits for them, and re-layouts  1.28 us (2%)
    pallas_call x1, Pallas kernels, per_device(): pl.pallas_call(kernel, out_shape=(jax.ShapeDtypeStruct((128, 256), BF), j...  79.4 us
    pallas_call x1, Pallas kernels, per_device(): pl.pallas_call(finish, out_shape=(shape, shape, shape, jax.ShapeDtypeStru...  3 us

profile of v5, /device:TPU:1, one launch (start us, length us, event | category | flops | bytes accessed | tf_op | source)
XLA Modules:
  0.0 84.5 jit_solution(9832386268634576643)
XLA Ops:
  0.6 0.0 copy-start
  0.6 0.0 copy-start.9
  0.7 0.0 copy-start.2
  0.7 0.0 copy-start.6
  0.7 0.0 copy-start.8
  0.7 0.0 copy-start.3
  0.7 0.0 copy-start.7
  0.7 0.0 copy-start.5
  0.7 0.0 copy-start.4
  0.7 1.2 %copy.18 = bf16[72,8,2,256]{3,1,2,0:T(8,128)(2,1)S(1)} copy(bf16[72,8,2,256]{3,2,1,0:T(2,128)(2,1)} %bitcast.18) | data formatting | bytes 1179648
  2.0 0.0 copy-done
  2.0 0.0 copy-done.9
  2.0 0.0 copy-done.2
  2.0 0.0 copy-done.6
  2.0 0.0 copy-done.8
  2.0 0.0 copy-done.3
  2.0 0.0 copy-done.7
  2.0 0.0 copy-done.5
  2.0 0.0 copy-done.4
  2.1 0.0 copy-start.1
  2.1 79.4 %shard_map.162 = (bf16[128,256]{1,0:T(8,128)(2,1)S(1)}, bf16[8,240,128]{2,1,0:T(8,128)(2,1)S(1)}, bf16[8,192,128]{2,1,0:T(8,128)(2,1)S(1)}, f32[8,128]{1,0:T(8,128)S(1)}) custom-call(s32[8]{0:T(128)S(1)} %copy-done.2, bf16[8,2,16,32]{3,2,1,0:T(8,128)(2,1)S(1)} %bitcast.14, bf16[8,2,16,32]{3,2,1,0:T(8,128)(2,1)S(1)} %bitcast.15, ...), custom_call_target="tpu_custom_call" | custom-call | flops 1000000000 | bytes 8000000 | tf_op jit(solution)/shard_map/pallas_call | solution.py:544
  81.4 0.0 copy-done.1
  81.5 3.0 %shard_map.163 = (bf16[8,2,16,32]{3,2,1,0:T(8,128)(2,1)}, bf16[8,2,16,32]{3,2,1,0:T(8,128)(2,1)}, bf16[8,2,16,32]{3,2,1,0:T(8,128)(2,1)}, f32[2,3,3,32,2,256]{5,...) custom-call(s32[8]{0:T(128)S(1)} %copy-done.2, ...), custom_call_target="tpu_custom_call" | custom-call | tf_op jit(solution)/shard_map/pallas_call | solution.py:564
Async XLA Ops:
  0.6 1.3 %copy-start = (bf16[512,512]{1,0:T(8,128)(2,1)S(1)}, bf16[512,512]{1,0:T(8,128)(2,1)}, u32[]{:S(2)}) copy-start(bf16[512,512]{1,0:T(8,128)(2,1)} %constant.6.clone.q5_ref) | copy-start | bytes 1572868
  0.6 1.3 %copy-start.9 = (bf16[128,128]{1,0:T(8,128)(2,1)S(1)}, bf16[128,128]{1,0:T(8,128)(2,1)}, u32[]{:S(2)}) copy-start(bf16[128,128]{1,0:T(8,128)(2,1)} %constant.7.clone.pm_ref) | copy-start | bytes 98308
  0.7 1.3 %copy-start.2 = (s32[8]{0:T(128)S(1)}, s32[8]{0:T(128)}, u32[]{:S(2)}) copy-start(s32[8]{0:T(128)} %reset_ref.3) | copy-start | bytes 100
  0.7 1.3 %copy-start.6 = (bf16[32,8,2,16]{0,3,2,1:T(8,128)(2,1)S(1)}, bf16[32,8,2,16]{0,3,2,1:T(8,128)(2,1)}, u32[]{:S(2)}) copy-start(bf16[32,8,2,16]{0,3,2,1:T(8,128)(2,1)} %param.18) | copy-start | bytes 49156
  0.7 1.3 %copy-start.8 = (f32[32]{0:T(128)S(1)}, f32[32]{0:T(128)}, u32[]{:S(2)}) copy-start(f32[32]{0:T(128)} %param.17) | copy-start | bytes 388
  0.7 1.3 %copy-start.3 = (bf16[2,3,3,32,256]{4,3,2,1,0:T(8,128)(2,1)S(1)}, bf16[2,3,3,32,256]{4,3,2,1,0:T(8,128)(2,1)}, u32[]{:S(2)}) copy-start(bf16[2,3,3,32,256]{4,3,2,1,0:T(8,128)(2,1)} %param.16) | copy-start | bytes 884740
  0.7 1.3 %copy-start.7 = (f32[2,32]{1,0:T(2,128)S(1)}, f32[2,32]{1,0:T(2,128)}, u32[]{:S(2)}) copy-start(f32[2,32]{1,0:T(2,128)} %gb_ref.1) | copy-start | bytes 772
  0.7 1.3 %copy-start.5 = (bf16[32,8,2,16]{0,3,2,1:T(8,128)(2,1)S(1)}, bf16[32,8,2,16]{0,3,2,1:T(8,128)(2,1)}, u32[]{:S(2)}) copy-start(bf16[32,8,2,16]{0,3,2,1:T(8,128)(2,1)} %param.12) | copy-start | bytes 49156
  0.7 1.3 %copy-start.4 = (bf16[32,8,2,16]{0,3,2,1:T(8,128)(2,1)S(1)}, bf16[32,8,2,16]{0,3,2,1:T(8,128)(2,1)}, u32[]{:S(2)}) copy-start(bf16[32,8,2,16]{0,3,2,1:T(8,128)(2,1)} %param.11) | copy-start | bytes 49156
  2.1 79.4 %copy-start.1 = (bf16[128,128]{1,0:T(8,128)(2,1)S(1)}, bf16[128,128]{1,0:T(8,128)(2,1)}, u32[]{:S(2)}) copy-start(bf16[128,128]{1,0:T(8,128)(2,1)} %constant.8.clone.pm_ref) | copy-start | bytes 98308
